TPU v7x, 32 devices: a whole 2x2x4 slice. The times are simulated.
32 devices in a mesh: seq: 4 (over z), chan: 8 (over y, x, core).
Axes of the slice: x: 2, y: 2, z: 4, core: 2. Of those that a mesh axis runs over, the one named last changes fastest.
Arguments:
- tokens: bfloat16 [2048, 4096], P('seq', 'chan'), may hold values from -6 to 6
- gate_proj: bfloat16 [4096, 8192], P(None, 'chan'), may hold values from -0.09375 to 0.09375
- value_proj: bfloat16 [4096, 8192], P(None, 'chan'), may hold values from -0.09375 to 0.09375
- state_proj: bfloat16 [4096, 256], replicated, may hold values from -0.0078125 to 0.0078125
- step_proj: bfloat16 [4096, 64], P(None, 'chan'), may hold values from -0.09375 to 0.09375
- step_bias: float32 [64], P('chan'), may hold values from -1 to 1
- decay_rate: float32 [64], P('chan'), may hold values from 0.0001 to 0.05
- skip_gain: float32 [64], P('chan'), may hold values from 0.5 to 4
- conv_kernel: float32 [4, 8192], P(None, 'chan'), may hold values from -3 to 3
- norm_gain: float32 [8192], P('chan'), may hold values from 0.1 to 1.9
- out_proj: bfloat16 [8192, 4096], P('chan'), may hold values from -0.046875 to 0.046875
- complement: int32 [4096], replicated, may hold values from 0 to 4095, as said below
- keep_mask: int32 [2048, 4096], P('seq', 'chan'), may hold values 0 or 1
Outputs:
- mixed: bfloat16 [2048, 4096], P('seq', 'chan')
Inputs may be any that keep to these rules, and one draw needn't show every extreme that they name: complement pairs the features: complement[complement[j]] = j and complement[j] != j for every j.
All inputs are finite; a program needn't handle non-finite values. No bound on the sum of `keep_mask` on one device may be relied on, other than what follows from the above.
Results may differ from a plain program's by a relative error of at most 0.025.
Values may be sent and summed in bfloat16 or wider, within the bound.
A program may use at most 128 MiB of HBM per device.

v0:
```python
import jax
import jax.numpy as jnp
from jax import lax
from jax.sharding import PartitionSpec as P

KW = 4
BLOCK = 256


def from_partner(block, axis, stride):
    count = lax.axis_size(axis)
    route = []
    for low in range(count):
        high = low | 1 << stride
        if high != low and high < count:
            route += [(low, high), (high, low)]
    return lax.ppermute(block, axis, route)


def from_behind(block, axis, distance):
    devices = range(lax.axis_size(axis))
    route = [(i - distance, i) for i in devices if i - distance in devices]
    return lax.ppermute(block, axis, route)


def entering_2(value, axis, join, neutral):
    place = lax.axis_index(axis)
    gathered = jax.tree.map(
        lambda a, kind: lax.all_gather(a.astype(kind), axis), value, (jnp.bfloat16, jnp.bfloat16)
    )
    state = jax.tree.map(lambda a, e: jnp.zeros_like(a) + jnp.asarray(e, a.dtype), value, neutral)

    def one(hop, state):
        return join(
            state,
            jax.tree.map(
                lambda a, own: lax.dynamic_index_in_dim(a, hop, 0, False).astype(own.dtype),
                gathered,
                value,
            ),
        )

    return lax.fori_loop(0, place, one, state)


def block_step(state, items):
    x_heads, b_part, c_part, step, log_decay = items
    cumulative = jnp.cumsum(log_decay, axis=1)
    gaps = cumulative[:, :, None, :] - cumulative[:, None, :, :]
    length = cumulative.shape[1]
    lower_mask = (jnp.arange(length)[:, None] >= jnp.arange(length)[None, :])[None, :, :, None]
    weights = jnp.where(lower_mask, jnp.exp(jnp.where(lower_mask, gaps, 0.0)), 0.0)
    x_float = x_heads.astype(jnp.float32)
    b_float = b_part.astype(jnp.float32)
    c_float = c_part.astype(jnp.float32)
    highest = lax.Precision.HIGHEST
    scores = jnp.einsum("btn,bsn->bts", c_float, b_float, precision=highest)
    mixing = weights * scores[..., None] * step[:, None, :, :]
    inner_y = jnp.einsum("btsh,bshp->bthp", mixing, x_float, precision=highest)
    carried = jnp.exp(cumulative)[..., None] * jnp.einsum(
        "btn,bhpn->bthp", c_float, state, precision=highest
    )
    total_decay = cumulative[:, -1, :]
    towards = jnp.exp(total_decay[:, None, :] - cumulative) * step
    fresh = jnp.einsum("bsh,bshp,bsn->bhpn", towards, x_float, b_float, precision=highest)
    new_state = jnp.exp(total_decay)[:, :, None, None] * state + fresh
    return (new_state, inner_y + carried)


def ssd_blocks(x_heads, b_part, c_part, step, log_decay):
    branches, length, heads, head_dim = x_heads.shape
    nblocks = length // BLOCK

    def blocked(arr):
        return jnp.moveaxis(arr.reshape((branches, nblocks, BLOCK) + arr.shape[2:]), 1, 0)

    start_state = jnp.zeros((branches, heads, head_dim, b_part.shape[-1]), jnp.float32)
    end_state, outputs = lax.scan(
        block_step,
        start_state,
        (blocked(x_heads), blocked(b_part), blocked(c_part), blocked(step), blocked(log_decay)),
    )
    return (jnp.moveaxis(outputs, 0, 1).reshape(x_heads.shape), end_state)


def combine_states(earlier, later):
    return (earlier[0] * later[0], later[0][..., None, None] * earlier[1] + later[1])


def mirror_rows(rows_block):
    nbits = lax.axis_size("seq").bit_length() - 1
    for bit_index in range(nbits):
        rows_block = from_partner(rows_block, "seq", bit_index)
    return rows_block[::-1]


def from_lower(tail):
    return from_behind(tail, "seq", 1)


def from_earlier(decays, states):
    identity = (jnp.ones_like(decays), jnp.zeros_like(states))
    return entering_2((decays, states), "seq", combine_states, identity)[1]


def shards(
    tokens,
    gate_proj,
    value_proj,
    state_proj,
    step_proj,
    step_bias,
    decay_rate,
    skip_gain,
    conv_kernel,
    norm_gain,
    out_proj,
    complement,
    keep_mask,
):
    rows = tokens.shape[0]
    inner = gate_proj.shape[1]
    heads = step_proj.shape[1]
    head_dim = inner // heads
    nstate = state_proj.shape[1] // 2
    width = gate_proj.shape[0]
    w_forward = jnp.concatenate([gate_proj, value_proj, state_proj, step_proj], axis=1)
    positions = jnp.arange(width, dtype=jnp.int32)
    inverse = jnp.zeros((width,), jnp.int32).at[complement].set(positions)
    w_reverse = jnp.take(w_forward, inverse, axis=0)
    mirrored = mirror_rows(tokens)
    first = jnp.dot(
        lax.all_gather(tokens, "chan", axis=1, tiled=True),
        w_forward,
        preferred_element_type=jnp.float32,
    )
    second = jnp.dot(
        lax.all_gather(mirrored, "chan", axis=1, tiled=True),
        w_reverse,
        preferred_element_type=jnp.float32,
    )
    proj = jnp.stack([first, second])
    gate_part = proj[..., :inner].astype(jnp.bfloat16)
    value_part = proj[..., inner : 2 * inner].astype(jnp.bfloat16)
    b_part = proj[..., 2 * inner : 2 * inner + nstate].astype(jnp.bfloat16)
    c_part = proj[..., 2 * inner + nstate : 2 * inner + 2 * nstate].astype(jnp.bfloat16)
    step_raw = proj[..., 2 * inner + 2 * nstate :]
    tail = value_part[:, rows - (KW - 1) :, :]
    before = from_lower(tail)
    padded = jnp.concatenate([before, value_part], axis=1).astype(jnp.float32)
    conv = conv_kernel[0] * padded[:, 0:rows, :]
    for tap in range(1, KW):
        conv = conv + conv_kernel[tap] * padded[:, tap : tap + rows, :]
    x_ssm = jax.nn.silu(conv).astype(jnp.bfloat16)
    step = jax.nn.softplus(step_raw + step_bias)
    log_decay = -step * decay_rate
    x_heads = x_ssm.reshape(2, rows, heads, head_dim)
    local_y, end_state = ssd_blocks(x_heads, b_part, c_part, step, log_decay)
    running = jnp.cumsum(log_decay, axis=1)
    shard_decay = jnp.exp(running[:, -1, :])
    incoming = from_earlier(shard_decay, end_state)
    entering = jnp.einsum(
        "btn,bhpn->bthp", c_part.astype(jnp.float32), incoming, precision=lax.Precision.HIGHEST
    )
    full_y = (
        local_y
        + jnp.exp(running)[..., None] * entering
        + skip_gain[:, None] * x_heads.astype(jnp.float32)
    )
    gated = full_y * jax.nn.silu(gate_part.astype(jnp.float32).reshape(2, rows, heads, head_dim))
    scale = lax.rsqrt(jnp.mean(gated * gated, axis=-1, keepdims=True) + 1e-05)
    normed = (
        (gated * scale * norm_gain.reshape(heads, head_dim))
        .reshape(2, rows, inner)
        .astype(jnp.bfloat16)
    )
    back_rows = mirror_rows(normed[1])
    stacked = jnp.concatenate([normed[0], back_rows], axis=1)
    out_table = jnp.concatenate([out_proj, jnp.take(out_proj, complement, axis=1)], axis=0)
    partial_total = jnp.dot(stacked, out_table, preferred_element_type=jnp.float32)
    summed = lax.psum_scatter(
        partial_total.astype(jnp.bfloat16), "chan", scatter_dimension=1, tiled=True
    ).astype(jnp.float32)
    return (summed * keep_mask.astype(jnp.float32) * (1.0 / 0.9)).astype(jnp.bfloat16)


def solution(mesh):
    return jax.shard_map(
        shards,
        mesh=mesh,
        in_specs=(
            P("seq", "chan"),
            P(None, "chan"),
            P(None, "chan"),
            P(),
            P(None, "chan"),
            P("chan"),
            P("chan"),
            P("chan"),
            P(None, "chan"),
            P("chan"),
            P("chan", None),
            P(),
            P("seq", "chan"),
        ),
        out_specs=P("seq", "chan"),
        check_vma=False,
    )
```

profile of v0, /device:TPU:0, one launch (start us, length us, event | category | flops | bytes accessed | tf_op | source)
XLA Modules:
  0.0 465.3 jit_solution(4568757348197060860)
XLA Ops:
  7.3 3.1 collective-permute-start
  10.4 12.1 %collective-permute-done = bf16[512,512]{1,0:T(8,128)(2,1)S(1)} collective-permute-done((bf16[512,512]{1,0:T(8,128)(2,1)}, bf16[512,512]{1,0:T(8,128)(2,1)S(1)}, u32[]{:S(2)}, u32[]{:S(2)}) %collective-permute-start) | collective-permute-done | bytes 524320 | tf_op jit(solution)/shard_map/ppermute | solution.py:17
  22.5 2.8 collective-permute-start.1
  25.3 22.5 %collective-permute-done.1 = bf16[512,512]{1,0:T(8,128)(2,1)S(1)} collective-permute-done((bf16[512,512]{1,0:T(8,128)(2,1)S(1)}, bf16[512,512]{1,0:T(8,128)(2,1)S(1)}, u32[]{:S(2)}, u32[]{:S(2)}) %collective-permute-start.1) | collective-permute-done | bytes 524320 | tf_op jit(solution)/shard_map/ppermute | solution.py:17
  47.8 5.1 %rev.6 = bf16[512,512]{1,0:T(8,128)(2,1)} reverse(bf16[512,512]{1,0:T(8,128)(2,1)S(1)} %collective-permute-done.1), dimensions={0} | reverse | bytes 1048576 | tf_op jit(solution)/shard_map/rev | solution.py:94
  55.6 15.5 %scatter_custom_fusion = s32[4096]{0:T(1024)S(1)} fusion(s32[4096]{0:T(1024)S(1)} %get-tuple-element.166, s32[4096]{0:T(1024)S(1)} %iota.19, s32[]{:T(128)} %constant.83.clone.1), kind=kCustom, calls=%fused_computation.111 | custom fusion | bytes 16388 | tf_op jit(solution)/shard_map/scatter | solution.py:129
  71.2 17.2 %pad_maximum_fusion = bf16[4096,2312]{1,0:T(8,128)(2,1)} fusion(bf16[4096,8]{1,0:T(8,128)(2,1)S(1)} %copy.66, bf16[4096,256]{1,0:T(8,128)(2,1)} %param.20, bf16[4096,1024]{1,0:T(8,128)(2,1)} %param.19, bf16[4096,1024]{1,0:T(8,128)(2,1)} %param.18), kind=kLoop, calls=%fused_computation.54 | loop fusion | flops 75759616 | bytes 37879808 | tf_op jit(solution)/shard_map/concatenate | solution.py:127
  88.4 46.1 %gather_fusion = bf16[4096,2312]{1,0:T(8,128)(2,1)} fusion(bf16[4096,2312]{1,0:T(8,128)(2,1)} %pad_maximum_fusion, s32[4096]{0:T(1024)S(1)} %fusion.71), kind=kCustom, calls=%fused_computation | custom fusion | bytes 37896192 | tf_op jit(solution)/shard_map/jit(_take)/gather | solution.py:130
  134.6 17.5 %convolution_bitcast_fusion = f32[1,512,2312]{1,2,0:T(8,128)} fusion(bf16[4096,2312]{1,0:T(8,128)(2,1)} %pad_maximum_fusion, bf16[512,4096]{1,0:T(8,128)(2,1)} %all-gather.6.cloned.1.call-done), kind=kOutput, calls=%fused_computation.72 | convolution fusion | flops 9697230848 | bytes 27869184 | tf_op jit(solution)/shard_map/dot_general | solution.py:132
  152.1 19.4 %fusion.54 = f32[1,512,2312]{1,2,0:T(8,128)} fusion(bf16[512,4096]{1,0:T(8,128)(2,1)} %all-gather.8.cloned.1.call-done, bf16[4096,2312]{1,0:T(8,128)(2,1)} %gather_fusion, pred[4096]{0:T(1024)(128)(4,1)S(1)} %compare_and_fusion.1), kind=kOutput, calls=%fused_computation.71 | convolution fusion | flops 9706700800 | bytes 27873280 | tf_op jit(solution)/shard_map/dot_general | solution.py:137
  171.5 4.5 fusion.50
  180.5 3.5 collective-permute-start.2
  189.5 5.3 %collective-permute-done.2 = bf16[2,3,1024]{1,2,0:T(8,128)(2,1)} collective-permute-done((bf16[2,3,1024]{1,2,0:T(8,128)(2,1)}, bf16[2,3,1024]{1,2,0:T(8,128)(2,1)}, u32[]{:S(2)}, u32[]{:S(2)}) %collective-permute-start.2) | collective-permute-done | bytes 12320 | tf_op jit(solution)/shard_map/ppermute | solution.py:23
  199.4 5.2 %multiply_convert_fusion.1 = bf16[2,512,1024]{1,2,0:T(8,128)(2,1)} fusion(f32[2,515,1024]{1,2,0:T(8,128)S(1)} %maximum_convert_fusion, f32[1024]{0:T(1024)S(1)} %bitcast.147, f32[1024]{0:T(1024)S(1)} %bitcast.149, f32[1024]{0:T(1024)S(1)} %bitcast.145, f32[1024]{0:T(1024)S(1)} %bitcast.143), kind=kLoop, calls=%fused_computation.88 | loop fusion | flops 12582912 | bytes 18890752 | tf_op jit(solution)/shard_map/convert_element_type | solution.py:154
  208.8 25.9 %while.26 = (s32[]{:T(128)}, f32[2,8,128,128]{3,2,1,0:T(8,128)S(1)}, f32[2,2,256,8,128]{2,4,3,1,0:T(8,128)}, f32[2,2,256,8]{2,3,1,0:T(8,128)S(1)}, f32[2,2,256,8...) while((s32[]{:T(128)}, ...), condition=%wide.region_4.5_spmd.clone, body=%wide.region_1.4_spmd.clone.sunk | while | flops 3263766528 | bytes 21895076 | solution.py:78
  211.7 4.8 %fusion.111 = f32[2,8,128,256]{3,2,1,0:T(8,128)S(1)} fusion(f32[2,256,8]{1,2,0:T(8,128)S(1)} %get-tuple-element.257, f32[2,256,256]{2,1,0:T(8,128)S(1)} %fusion.110, f32[2,256,8]{1,2,0:T(8,128)S(1)} %get-tuple-element.255, pred[256,256]{1,0:T(8,128)(4,1)S(1)} %iota_compare_fusion.2, bf16[2,2,256,8,128]{2,4,3,1,0:T(8,128)(2,1)} %get-tuple-element.286, ...), kind=kOutput, calls=%fused_computation.5.clone.1 | convolution fusion | flops 1615855616 | bytes 3785216 | tf_op jit(solution)/shard_map/while/body/eval_jaxpr/btsh,bshp->bthp/dot_general | solution.py:59
  216.5 3.5 bitcast_dynamic-update-slice_fusion.2
  224.7 4.8 %fusion.111 = f32[2,8,128,256]{3,2,1,0:T(8,128)S(1)} fusion(f32[2,256,8]{1,2,0:T(8,128)S(1)} %get-tuple-element.257, f32[2,256,256]{2,1,0:T(8,128)S(1)} %fusion.110, f32[2,256,8]{1,2,0:T(8,128)S(1)} %get-tuple-element.255, pred[256,256]{1,0:T(8,128)(4,1)S(1)} %iota_compare_fusion.2, bf16[2,2,256,8,128]{2,4,3,1,0:T(8,128)(2,1)} %get-tuple-element.286, ...), kind=kOutput, calls=%fused_computation.5.clone.1 | convolution fusion | flops 1615855616 | bytes 3785216 | tf_op jit(solution)/shard_map/while/body/eval_jaxpr/btsh,bshp->bthp/dot_general | solution.py:59
  229.5 3.5 bitcast_dynamic-update-slice_fusion.2
  238.6 12.9 %all-gather = bf16[8,1,8]{2,1,0:T(2,128)(2,1)S(1)} all-gather(bf16[2,1,8]{2,1,0:T(2,128)(2,1)S(1)} %copy.75), channel_id=2, replica_groups=mesh['seq'=4,'chan'=8] {'seq'}, dimensions={0}, use_global_device_ids=true | all-gather | bytes 160 | tf_op jit(solution)/shard_map/all_gather | solution.py:29
  251.9 4.9 %copy.86 = f32[2,2,8,16,8,256]{5,4,0,3,2,1:T(8,128)} copy(f32[2,2,8,16,8,256]{5,4,3,2,1,0:T(8,128)} %bitcast.135) | data formatting | bytes 8388608 | tf_op jit(solution)/shard_map/reshape | solution.py:83
  256.8 28.0 %all-gather.10.cloned.1.call-done = bf16[8,8,128,128]{3,2,1,0:T(8,128)(2,1)} async-done(((bf16[2,8,128,128]{3,2,1,0:T(8,128)(2,1)}), bf16[8,8,128,128]{3,2,1,0:T(8,128)(2,1)}) %all-gather.10.cloned.1.call-update) | async-done | bytes 2097168 | tf_op jit(solution)/shard_map/all_gather | solution.py:29
  285.0 2.9 fusion.68
  287.9 9.8 %multiply_reduce_fusion = (f32[2,512,8]{1,2,0:T(8,128)S(1)}, f32[2,512,8,128]{1,3,2,0:T(8,128)S(1)}) fusion(f32[8]{0:T(128)S(1)} %copy-done.16, f32[2,512,8,128]{1,3,2,0:T(8,128)S(1)} %bitcast.133, f32[2,512,8,128]{1,3,2,0:T(8,128)S(1)} %fusion.68, f32[2,512,8]{1,2,0:T(8,128)S(1)} %copy.74, bf16[2,512,1024]{1,2,0:T(8,128)(2,1)S(1)} %copy-done.6, ...), kind=kLoop, calls=%fused_computation.87 | loop fusion | flops 26206208 | bytes 31539232 | tf_op jit(solution)/shard_map/reduce_sum | solution.py:171
  299.9 12.0 %copy.78 = bf16[1024,4096]{0,1:T(8,128)(2,1)} copy(bf16[1024,4096]{1,0:T(8,128)(2,1)} %param.27) | data formatting | bytes 16777216 | tf_op args[10]
  311.9 25.4 %gather_fusion.1 = bf16[4096,1024]{1,0:T(8,128)(2,1)} fusion(bf16[1024,4096]{0,1:T(8,128)(2,1)} %copy.78, s32[4096]{0:T(1024)S(1)} %copy-done.8), kind=kCustom, calls=%fused_computation.1 | custom fusion | bytes 16793600 | tf_op jit(solution)/shard_map/jit(_take)/gather | solution.py:179
  337.3 4.6 collective-permute-start.4
  341.9 7.3 %select_bitcast_fusion = bf16[1024,4096]{0,1:T(8,128)(2,1)} fusion(bf16[4096,1024]{1,0:T(8,128)(2,1)} %gather_fusion.1, pred[4096]{0:T(1024)(128)(4,1)S(1)} %compare_and_fusion), kind=kLoop, calls=%fused_computation.67 | loop fusion | flops 4194304 | bytes 16781312 | tf_op jit(solution)/shard_map/jit(_take)/select_n | solution.py:179
  349.1 38.3 %collective-permute-done.4 = bf16[512,1024]{0,1:T(8,128)(2,1)S(1)} collective-permute-done((bf16[512,1024]{0,1:T(8,128)(2,1)}, bf16[512,1024]{0,1:T(8,128)(2,1)S(1)}, u32[]{:S(2)}, u32[]{:S(2)}) %collective-permute-start.4) | collective-permute-done | bytes 1048608 | tf_op jit(solution)/shard_map/ppermute | solution.py:17
  387.4 3.2 rev.7
  390.7 14.0 %fusion.51 = bf16[512,4096]{1,0:T(8,128)(2,1)} fusion(bf16[1024,4096]{0,1:T(8,128)(2,1)} %select_bitcast_fusion, bf16[1024,4096]{0,1:T(8,128)(2,1)} %copy.78, bf16[512,1024]{0,1:T(8,128)(2,1)S(1)} %rev.7, bf16[512,1024]{0,1:T(8,128)(2,1)S(1)} %bitcast.138), kind=kOutput, calls=%fused_computation.68 | convolution fusion | flops 8629780480 | bytes 23068672 | tf_op jit(solution)/shard_map/dot_general | solution.py:180
  404.6 51.7 %reduce-scatter.2.cloned.1.call-done = bf16[512,512]{1,0:T(8,128)(2,1)} async-done(((bf16[512,4096]{1,0:T(8,128)(2,1)}), bf16[512,512]{1,0:T(8,128)(2,1)}) %reduce-scatter.2.cloned.1.call-update) | async-done | bytes 524304 | tf_op jit(solution)/shard_map/reduce_scatter | solution.py:181
  (111 shorter events, 39.9 us)
Async XLA Ops:
  6.5 128.1 %all-gather.6.cloned.1.call-start = ((), (), s32[]{:S(2)}) async-start(), calls=%async_computation.1 | async-start | bytes 4718592 | tf_op jit(solution)/shard_map/all_gather | solution.py:133
  7.3 144.9 %all-gather.8.cloned.1.call-start = ((), (), s32[]{:S(2)}) async-start(), calls=%async_computation.2 | async-start | bytes 4718592 | tf_op jit(solution)/shard_map/all_gather | solution.py:138
  7.3 15.2 %collective-permute-start = (bf16[512,512]{1,0:T(8,128)(2,1)}, bf16[512,512]{1,0:T(8,128)(2,1)S(1)}, u32[]{:S(2)}, u32[]{:S(2)}) collective-permute-start(bf16[512,512]{1,0:T(8,128)(2,1)} %param.17), channel_id=1, source_target_pairs={{0,8},{8,0},{16,24},{24,16},{1,9},{9,1},{17,25},{25,17},{2,10},{10... | collective-permute-start | bytes 1572872 | tf_op jit(solution)/shard_map/ppermute | solution.py:17
  22.5 25.2 %collective-permute-start.1 = (bf16[512,512]{1,0:T(8,128)(2,1)S(1)}, bf16[512,512]{1,0:T(8,128)(2,1)S(1)}, u32[]{:S(2)}, u32[]{:S(2)}) collective-permute-start(bf16[512,512]{1,0:T(8,128)(2,1)S(1)} %collective-permute-done), channel_id=1, source_target_pairs={{0,16},{16,0},{8,24},{24,8},{1,17},{17,1},{9,25},{25,9},{2,18},{18... | collective-permute-start | bytes 1572872 | tf_op jit(solution)/shard_map/ppermute | solution.py:17
  52.9 231.9 %all-gather.10.cloned.1.call-start = ((), (), s32[]{:S(2)}) async-start(), calls=%async_computation.4 | async-start | bytes 2621440 | tf_op jit(solution)/shard_map/all_gather | solution.py:29
  88.4 46.2 %copy-start.12 = (f32[4,1024]{1,0:T(4,128)S(1)}, f32[4,1024]{1,0:T(4,128)}, u32[]{:S(2)}) copy-start(f32[4,1024]{1,0:T(4,128)} %param.25) | copy-start | bytes 49156
  134.6 62.5 %copy-start.10 = (f32[1,1024]{1,0:T(1,128)}, f32[1,1024]{1,0:T(1,128)S(1)}, u32[]{:S(2)}) copy-start(f32[1,1024]{1,0:T(1,128)S(1)} %get-tuple-element.165) | copy-start | bytes 12292
  176.1 3.7 copy-start.2
  176.1 7.9 %copy-start.3 = (f32[1,512,2312]{1,2,0:T(8,128)S(1)}, f32[1,512,2312]{1,2,0:T(8,128)}, u32[]{:S(2)}) copy-start(f32[1,512,2312]{1,2,0:T(8,128)} %convolution_bitcast_fusion) | copy-start | bytes 14204932
  176.1 7.9 %copy-start.4 = (f32[1,512,2312]{1,2,0:T(8,128)S(1)}, f32[1,512,2312]{1,2,0:T(8,128)}, u32[]{:S(2)}) copy-start(f32[1,512,2312]{1,2,0:T(8,128)} %fusion.54) | copy-start | bytes 14204932
  176.1 7.9 %copy-start.14 = (f32[8]{0:T(128)S(1)}, f32[8]{0:T(128)}, u32[]{:S(2)}) copy-start(f32[8]{0:T(128)} %param.23) | copy-start | bytes 100
  176.1 7.9 %copy-start.15 = (f32[8]{0:T(128)S(1)}, f32[8]{0:T(128)}, u32[]{:S(2)}) copy-start(f32[8]{0:T(128)} %param.22) | copy-start | bytes 100
  180.5 14.3 %collective-permute-start.2 = (bf16[2,3,1024]{1,2,0:T(8,128)(2,1)}, bf16[2,3,1024]{1,2,0:T(8,128)(2,1)}, u32[]{:S(2)}, u32[]{:S(2)}) collective-permute-start(bf16[2,3,1024]{1,2,0:T(8,128)(2,1)} %slice.104), channel_id=1, source_target_pairs={{0,8},{8,16},{16,24},{1,9},{9,17},{17,25},{2,10},{10,18},{18,26},{... | collective-permute-start | bytes 36872 | tf_op jit(solution)/shard_map/ppermute | solution.py:23
  197.1 2.3 copy-start
  216.5 3.5 copy-start.1
  229.5 3.5 copy-start.1
  235.7 220.6 %reduce-scatter.2.cloned.1.call-start = ((), (), s32[]{:S(2)}) async-start(), calls=%async_computation.3 | async-start | bytes 4718592 | tf_op jit(solution)/shard_map/reduce_scatter | solution.py:181
  284.9 3.0 copy-start.6
  284.9 3.0 copy-start.5
  284.9 3.0 copy-start.11
  285.0 3.0 copy-start.16
  287.9 9.8 %copy-start.13 = (f32[1024]{0:T(1024)S(1)}, f32[1024]{0:T(1024)}, u32[]{:S(2)}) copy-start(f32[1024]{0:T(1024)} %param.26) | copy-start | bytes 12292
  298.6 13.3 %copy-start.8 = (s32[4096]{0:T(1024)S(1)}, s32[4096]{0:T(1024)}, u32[]{:S(2)}) copy-start(s32[4096]{0:T(1024)} %get-tuple-element.167) | copy-start | bytes 49156
  298.6 38.7 %collective-permute-start.3 = (bf16[512,1024]{0,1:T(8,128)(2,1)S(1)}, bf16[512,1024]{0,1:T(8,128)(2,1)}, u32[]{:S(2)}, u32[]{:S(2)}) collective-permute-start(bf16[512,1024]{0,1:T(8,128)(2,1)S(1)} %bitcast.139), channel_id=1, source_target_pairs={{0,8},{8,0},{16,24},{24,16},{1,9},{9,1},{17,25},{25,17},{2,10},{10... | collective-permute-start | bytes 3145736 | tf_op jit(solution)/shard_map/ppermute | solution.py:17
  311.9 25.4 %copy-start.9 = (s32[4096]{0:T(1024)S(1)}, s32[4096]{0:T(1024)}, u32[]{:S(2)}) copy-start(s32[4096]{0:T(1024)} %param.28) | copy-start | bytes 49156
  337.3 50.1 %collective-permute-start.4 = (bf16[512,1024]{0,1:T(8,128)(2,1)}, bf16[512,1024]{0,1:T(8,128)(2,1)S(1)}, u32[]{:S(2)}, u32[]{:S(2)}) collective-permute-start(bf16[512,1024]{0,1:T(8,128)(2,1)} %collective-permute-done.3), channel_id=1, source_target_pairs={{0,16},{16,0},{8,24},{24,8},{1,17},{17,1},{9,25},{25,9},{2,18},{18... | collective-permute-start | bytes 3145736 | tf_op jit(solution)/shard_map/ppermute | solution.py:17
  404.6 51.7 %copy-start.7 = (s32[512,512]{1,0:T(8,128)S(1)}, s32[512,512]{1,0:T(8,128)}, u32[]{:S(2)}) copy-start(s32[512,512]{1,0:T(8,128)} %param.29) | copy-start | bytes 3145732
Sparse Core Ops, SparseCore 0:
  9.2 40.1 all-gather.5
  53.0 38.5 all-gather.7
  235.8 48.9 all-gather.9
  404.8 51.5 reduce-scatter.1
where the time goes:
time: 475 us; the launch traced here: 465 us
  waiting for transfers between devices  159 us (33%)
  local copies, waits for them, and re-layouts  132 us (28%)
  matrix products  76.2 us (16%)
  other arithmetic  56.3 us (12%)
  starting transfers between devices  15.3 us (3%)
  between operations  13.9 us (3%)
  blocking collectives  12.9 us (3%)
    ppermute x4, waiting for transfers between devices, from_partner(): return lax.ppermute(block, axis, route)  72.9 us
    reduce_scatter x1, waiting for transfers between devices, shards(): lax.psum_scatter(partial_total.astype(jnp.bfloat16), 'chan', scatter_dime...  51.7 us
    gather x1, local copies, waits for them, and re-layouts, shards(): w_reverse = jnp.take(w_forward, inverse, axis=0)  46.1 us
    all_gather x1, waiting for transfers between devices, entering_2(): lax.all_gather(a.astype(kind), axis)  28 us
    gather x1, local copies, waits for them, and re-layouts, shards(): jnp.take(out_proj, complement, axis=1)  25.4 us
    dot_general x1, matrix products, shards(): jnp.dot(lax.all_gather(mirrored, 'chan', axis=1, tiled=True), w_reverse,...  19.4 us
    dot_general x1, matrix products, shards(): jnp.dot(lax.all_gather(tokens, 'chan', axis=1, tiled=True), w_forward, pr...  17.5 us
    concatenate x1, other arithmetic, shards(): jnp.concatenate([gate_proj, value_proj, state_proj, step_proj], axis=1)  17.2 us
  transfers between devices with their start and end apart: 9, of which 6 were waited for; matrix products, arithmetic and copies ran while one was open for 35% of the time, Pallas kernels for 0%

commit v1 on v0

v1 whole, which is shorter than its diff:
```python
import functools

import jax
import jax.numpy as jnp
from jax import lax
from jax.experimental import pallas as pl
from jax.experimental.pallas import tpu as pltpu
from jax.sharding import PartitionSpec as P

KW = 4
HALO = 16
TILE = 256
F32 = jnp.float32
BF16 = jnp.bfloat16
VMEM_LIMIT = 50 * 1024 * 1024


def params(grid_rank):
    return pltpu.CompilerParams(
        dimension_semantics=("arbitrary",) * grid_rank, vmem_limit_bytes=VMEM_LIMIT
    )


def permute_body(a_ref, partner_ref, out_ref):
    width = a_ref.shape[1]
    tile = out_ref.shape[1]
    depth = min(1024, width)
    total = jnp.zeros(out_ref.shape, F32)
    for low in range(0, width, depth):
        source = lax.broadcasted_iota(jnp.int32, (depth, tile), 0) + low
        chosen = jnp.where(source == partner_ref[...], 1.0, 0.0).astype(BF16)
        total += jnp.dot(a_ref[:, low : low + depth], chosen, preferred_element_type=F32)
    out_ref[...] = total.astype(BF16)


def permute_columns(a, partner):
    rows, width = a.shape
    tile = 512
    return pl.pallas_call(
        permute_body,
        grid=(width // tile,),
        in_specs=[
            pl.BlockSpec((rows, width), lambda j: (0, 0)),
            pl.BlockSpec((1, tile), lambda j: (0, j)),
        ],
        out_specs=pl.BlockSpec((rows, tile), lambda j: (0, j)),
        out_shape=jax.ShapeDtypeStruct((rows, width), BF16),
        compiler_params=params(1),
        cost_estimate=pl.CostEstimate(
            flops=2 * rows * width * width, bytes_accessed=4 * rows * width, transcendentals=0
        ),
    )(a, partner)


def column_of(ref, head):
    values = ref[...]
    lanes = lax.broadcasted_iota(jnp.int32, values.shape, 1)
    return jnp.sum(jnp.where(lanes == head, values, 0.0), axis=1, keepdims=True)


def state_body(value_ref, halo_ref, taps_ref, b_ref, step_ref, cum_ref, xs_ref, state_ref):
    branch, head = pl.program_id(0), pl.program_id(1)
    rows = value_ref.shape[0]
    nstate = b_ref.shape[1]
    value = value_ref[...].astype(F32)
    halo = halo_ref[...].astype(F32)
    step = column_of(step_ref, head)
    cum = column_of(cum_ref, head)

    def finish(conv, end):
        xs = (conv / (1.0 + jnp.exp(-conv))).astype(BF16)
        xs_ref[...] = xs
        weighted = (xs.astype(F32) * (jnp.exp(end - cum) * step)).astype(BF16)
        state = lax.dot_general(
            b_ref[...], weighted, (((0,), (0,)), ((), ())), preferred_element_type=F32
        )
        state_ref[0, 0, :nstate, :] = state.astype(BF16)
        state_ref[0, 0, nstate:, :] = jnp.broadcast_to(
            jnp.exp(end), (HALO, state.shape[1])
        ).astype(BF16)

    @pl.when(branch == 0)
    def _():
        ext = jnp.concatenate([halo, value], axis=0)
        conv = taps_ref[KW - 1 : KW, :] * value
        for k in range(KW - 1):
            low = HALO - (KW - 1) + k
            conv += taps_ref[k : k + 1, :] * ext[low : low + rows]
        finish(conv, cum[rows - 1 : rows])

    @pl.when(branch == 1)
    def _():
        ext = jnp.concatenate([value, halo], axis=0)
        conv = taps_ref[KW - 1 : KW, :] * value
        for k in range(KW - 1):
            low = KW - 1 - k
            conv += taps_ref[k : k + 1, :] * ext[low : low + rows]
        finish(conv, cum[0:1])


def local_body(skip_ref, xs_ref, b_ref, c_ref, cum_ref, step_row_ref, cum_row_ref, y_ref, scores):
    branch, head = pl.program_id(0), pl.program_id(1)
    rows = xs_ref.shape[0]

    @pl.when(head == 0)
    def _():
        scores[...] = lax.dot_general(
            c_ref[...], b_ref[...], (((1,), (1,)), ((), ())), preferred_element_type=F32
        )

    cum = column_of(cum_ref, head)
    cum_row = cum_row_ref[0]
    step_row = step_row_ref[0]
    xs = xs_ref[...]
    skip = skip_ref[head]
    size = min(TILE, rows)
    below = lax.broadcasted_iota(jnp.int32, (size, size), 0) - lax.broadcasted_iota(
        jnp.int32, (size, size), 1
    )

    def run(sign):
        for t in range(0, rows, size):
            at = slice(t, t + size)
            total = xs[at].astype(F32) * skip
            for s in range(0, rows, size):
                if sign * (t - s) < 0:
                    continue
                gaps = cum[at] - cum_row[:, s : s + size]
                if s == t:
                    gaps = jnp.where(sign * below >= 0, gaps, -jnp.inf)
                mixing = jnp.exp(gaps) * (scores[at, s : s + size] * step_row[:, s : s + size])
                total += jnp.dot(
                    mixing.astype(BF16), xs[s : s + size], preferred_element_type=F32
                )
            y_ref[at, :] = total

    @pl.when(branch == 0)
    def _():
        run(1)

    @pl.when(branch == 1)
    def _():
        run(-1)


def norm_body(y_ref, c_ref, cum_ref, gate_ref, gain_ref, enter_ref, out_ref):
    head = pl.program_id(1)
    cum = column_of(cum_ref, head)
    carried = jnp.dot(c_ref[...], enter_ref[0, 0], preferred_element_type=F32)
    y = y_ref[...] + jnp.exp(cum) * carried
    gate = gate_ref[...].astype(F32)
    gated = y * (gate / (1.0 + jnp.exp(-gate)))
    mean = jnp.mean(gated * gated, axis=1, keepdims=True)
    out_ref[...] = (gated * lax.rsqrt(mean + 1e-05) * gain_ref[...]).astype(BF16)


def shift(block, distance):
    count = lax.axis_size("seq")
    route = [(i, i + distance) for i in range(count) if 0 <= i + distance < count]
    return lax.ppermute(block, "seq", route)


def entering(packed, nstate):
    count = lax.axis_size("seq")
    place = lax.axis_index("seq")
    gathered = lax.all_gather(packed, "seq")
    ends = gathered[:, :, :, :nstate, :].astype(F32)
    decays = gathered[:, :, :, nstate : nstate + 1, :].astype(F32)
    ahead = jnp.zeros(ends.shape[2:], F32)
    for z in range(count):
        ahead = jnp.where(z < place, decays[z, 0] * ahead + ends[z, 0], ahead)
    behind = jnp.zeros(ends.shape[2:], F32)
    for z in reversed(range(count)):
        behind = jnp.where(z > place, decays[z, 1] * behind + ends[z, 1], behind)
    return jnp.stack([ahead, behind]).astype(BF16)


def shards(
    tokens,
    gate_proj,
    value_proj,
    state_proj,
    step_proj,
    step_bias,
    decay_rate,
    skip_gain,
    conv_kernel,
    norm_gain,
    out_proj,
    complement,
    keep_mask,
):
    rows = tokens.shape[0]
    inner = gate_proj.shape[1]
    heads = step_proj.shape[1]
    head_dim = inner // heads
    nstate = state_proj.shape[1] // 2
    partner = complement[None, :]
    half = rows // 2

    parts = [
        lax.all_gather(tokens[low : low + half], "chan", axis=1, tiled=True)
        for low in (0, half)
    ]
    out_perm = permute_columns(out_proj, partner)
    swapped = [permute_columns(part, partner) for part in parts]
    both = jnp.concatenate(parts + swapped, axis=0)

    def project(weights):
        return jnp.dot(both, weights, preferred_element_type=F32)

    value = project(value_proj).astype(BF16)
    halo = jnp.concatenate(
        [shift(value[rows - HALO : rows], 1), shift(value[rows : rows + HALO], -1)], axis=0
    )
    bc = project(state_proj).astype(BF16)
    step = jax.nn.softplus(project(step_proj) + step_bias).reshape(2, rows, heads)
    log_decay = -step * decay_rate
    cum = jnp.stack(
        [jnp.cumsum(log_decay[0], axis=0), lax.cumsum(log_decay[1], axis=0, reverse=True)]
    )
    step_rows = jnp.swapaxes(step, 1, 2).reshape(2 * heads, 1, rows)
    cum_rows = jnp.swapaxes(cum, 1, 2).reshape(2 * heads, 1, rows)
    step = step.reshape(2 * rows, heads)
    cum = cum.reshape(2 * rows, heads)
    gate = project(gate_proj).astype(BF16)

    grid = (2, heads)
    block = pl.BlockSpec((rows, head_dim), lambda b, h: (b, h))
    b_block = pl.BlockSpec((rows, nstate), lambda b, h: (b, 0))
    c_block = pl.BlockSpec((rows, nstate), lambda b, h: (b, 1))
    column = pl.BlockSpec((rows, heads), lambda b, h: (b, 0))
    row = pl.BlockSpec((1, 1, rows), lambda b, h: (b * heads + h, 0, 0))

    xs, packed = pl.pallas_call(
        state_body,
        grid=grid,
        in_specs=[
            block,
            pl.BlockSpec((HALO, head_dim), lambda b, h: (b, h)),
            pl.BlockSpec((KW, head_dim), lambda b, h: (0, h)),
            b_block,
            column,
            column,
        ],
        out_specs=[
            block,
            pl.BlockSpec((1, 1, nstate + HALO, head_dim), lambda b, h: (b, h, 0, 0)),
        ],
        out_shape=[
            jax.ShapeDtypeStruct((2 * rows, inner), BF16),
            jax.ShapeDtypeStruct((2, heads, nstate + HALO, head_dim), BF16),
        ],
        compiler_params=params(2),
    )(value, halo, conv_kernel, bc, step, cum)

    enter = entering(packed, nstate)

    y = pl.pallas_call(
        local_body,
        grid=grid,
        in_specs=[
            pl.BlockSpec(memory_space=pltpu.SMEM),
            block,
            b_block,
            c_block,
            column,
            row,
            row,
        ],
        out_specs=block,
        out_shape=jax.ShapeDtypeStruct((2 * rows, inner), F32),
        scratch_shapes=[pltpu.VMEM((rows, rows), F32)],
        compiler_params=params(2),
        cost_estimate=pl.CostEstimate(
            flops=8 * rows * rows * inner,
            bytes_accessed=16 * rows * inner,
            transcendentals=2 * heads * rows * rows,
        ),
    )(skip_gain, xs, bc, bc, cum, step_rows, cum_rows)

    normed = pl.pallas_call(
        norm_body,
        grid=grid,
        in_specs=[
            block,
            c_block,
            column,
            block,
            pl.BlockSpec((1, head_dim), lambda b, h: (0, h)),
            pl.BlockSpec((1, 1, nstate, head_dim), lambda b, h: (b, h, 0, 0)),
        ],
        out_specs=pl.BlockSpec((rows, head_dim), lambda b, h: (0, b * heads + h)),
        out_shape=jax.ShapeDtypeStruct((rows, 2 * inner), BF16),
        compiler_params=params(2),
    )(y, bc, cum, gate, norm_gain[None, :], enter)

    table = jnp.concatenate([out_proj, out_perm], axis=0)
    results = []
    for low in (0, half):
        partial = jnp.dot(normed[low : low + half], table, preferred_element_type=F32)
        summed = lax.psum_scatter(
            partial.astype(BF16), "chan", scatter_dimension=1, tiled=True
        ).astype(F32)
        kept = keep_mask[low : low + half].astype(F32)
        results.append((summed * kept * (1.0 / 0.9)).astype(BF16))
    return jnp.concatenate(results, axis=0)


def solution(mesh):
    return jax.shard_map(
        shards,
        mesh=mesh,
        in_specs=(
            P("seq", "chan"),
            P(None, "chan"),
            P(None, "chan"),
            P(),
            P(None, "chan"),
            P("chan"),
            P("chan"),
            P("chan"),
            P(None, "chan"),
            P("chan"),
            P("chan", None),
            P(),
            P("seq", "chan"),
        ),
        out_specs=P("seq", "chan"),
        check_vma=False,
    )
```

time: 475 us -> 322 us (0.68); the launches traced: 465 us -> 321 us
  local copies, waits for them, and re-layouts: 132 us -> 6.14 us
  Pallas kernels: 0 us -> 103 us
  other arithmetic: 56.3 us -> 11.9 us
  waiting for transfers between devices: 159 us -> 125 us
  matrix products: 76.2 us -> 56.4 us
  blocking collectives: 12.9 us -> 0 us
  starting transfers between devices: 15.3 us -> 5.01 us
    pallas_call x0 -> x6, Pallas kernels: none -> 103 us  [the longest x3 64.5 us: permute_columns(): pl.pallas_call(permute_body, grid=(width // tile,), in_specs=[pl.BlockSpe...]
    ppermute x5 -> x2, waiting for transfers between devices: 78.2 us -> 0.05 us  [shift(): return lax.ppermute(block, 'seq', route)]
    gather x2 -> x0, local copies, waits for them, and re-layouts: 71.5 us -> none  [the longest x1 46.1 us: shards(): w_reverse = jnp.take(w_forward, inverse, axis=0)]
    reduce_scatter x1 -> x2, waiting for transfers between devices: 51.7 us -> 77.5 us  [shards(): lax.psum_scatter(partial.astype(BF16), 'chan', scatter_dimension=1, tiled...]
    dot_general x12 -> x6, matrix products: 76.2 us -> 56.4 us  [the longest x4 38.9 us: project(): return jnp.dot(both, weights, preferred_element_type=F32)]
    all_gather x3, waiting for transfers between devices: 28 us -> 47 us  [the longest x2 47 us: shards(): lax.all_gather(tokens[low:low + half], 'chan', axis=1, tiled=True)]
    concatenate x1 -> x2, other arithmetic: 17.2 us -> 0.83 us  [the longest x1 0.83 us: shards(): return jnp.concatenate(results, axis=0)]
    scatter x1 -> x0, local copies, waits for them, and re-layouts: 15.5 us -> none  [shards(): inverse = jnp.zeros((width,), jnp.int32).at[complement].set(positions)]
  transfers between devices with their start and end apart: 9 -> 7, of which waited for: 6 -> 4; matrix products, arithmetic and copies ran while one was open for 35% -> 10% of each run, Pallas kernels for 0% -> 20%
where the time goes in v1:
time: 322 us; the launch traced here: 321 us
  waiting for transfers between devices  125 us (39%)
  Pallas kernels  103 us (32%)
  matrix products  56.4 us (18%)
  between operations  13.5 us (4%)
  other arithmetic  11.9 us (4%)
  local copies, waits for them, and re-layouts  6.14 us (2%)
  starting transfers between devices  5.01 us (2%)
    reduce_scatter x2, waiting for transfers between devices, shards(): lax.psum_scatter(partial.astype(BF16), 'chan', scatter_dimension=1, tiled...  77.5 us
    pallas_call x3, Pallas kernels, permute_columns(): pl.pallas_call(permute_body, grid=(width // tile,), in_specs=[pl.BlockSpe...  64.5 us
    all_gather x2, waiting for transfers between devices, shards(): lax.all_gather(tokens[low:low + half], 'chan', axis=1, tiled=True)  47 us
    dot_general x4, matrix products, project(): return jnp.dot(both, weights, preferred_element_type=F32)  38.9 us
    dot_general x2, matrix products, shards(): partial = jnp.dot(normed[low:low + half], table, preferred_element_type=F32)  17.5 us
    pallas_call x1, Pallas kernels, shards(): pl.pallas_call(state_body, grid=grid, in_specs=[block, pl.BlockSpec((HALO...  14.5 us
    pallas_call x1, Pallas kernels, shards(): pl.pallas_call(norm_body, grid=grid, in_specs=[block, c_block, column, bl...  12 us
    pallas_call x1, Pallas kernels, shards(): pl.pallas_call(local_body, grid=grid, in_specs=[pl.BlockSpec(memory_space...  11.9 us
  transfers between devices with their start and end apart: 7, of which 4 were waited for; matrix products, arithmetic and copies ran while one was open for 10% of the time, Pallas kernels for 20%

profile of v1, /device:TPU:0, one launch (start us, length us, event | category | flops | bytes accessed | tf_op | source)
XLA Modules:
  0.0 321.2 jit_solution(2070506907884477290)
XLA Ops:
  6.5 2.0 fusion.28
  8.6 0.7 all-gather.5.cloned.1.call-update
  9.4 30.8 %all-gather.7.cloned.1.call-done.a_ref = bf16[256,4096]{1,0:T(8,128)(2,1)} async-done(((bf16[256,512]{1,0:T(8,128)(2,1)}), bf16[256,4096]{1,0:T(8,128)(2,1)}) %all-gather.7.cloned.1.call-update) | async-done | bytes 2097168 | tf_op jit(solution)/shard_map/all_gather | solution.py:202
  40.2 0.7 copy-done.6
  40.9 11.9 %shard_map.128 = bf16[256,4096]{1,0:T(8,128)(2,1)S(1)} custom-call(bf16[256,4096]{1,0:T(8,128)(2,1)} %all-gather.7.cloned.1.call-done.a_ref, s32[1,4096]{1,0:T(1,128)S(1)} %bitcast.113), custom_call_target="tpu_custom_call" | custom-call | flops 8589934592 | bytes 4194304 | tf_op jit(solution)/shard_map/pallas_call | solution.py:39
  52.8 1.3 copy-done.9
  54.1 16.2 %all-gather.5.cloned.1.call-done.a_ref = bf16[256,4096]{1,0:T(8,128)(2,1)} async-done(((bf16[256,512]{1,0:T(8,128)(2,1)}), bf16[256,4096]{1,0:T(8,128)(2,1)}) %all-gather.5.cloned.1.call-update) | async-done | bytes 2097168 | tf_op jit(solution)/shard_map/all_gather | solution.py:202
  70.3 12.1 %shard_map.127 = bf16[256,4096]{1,0:T(8,128)(2,1)S(1)} custom-call(bf16[256,4096]{1,0:T(8,128)(2,1)} %all-gather.5.cloned.1.call-done.a_ref, s32[1,4096]{1,0:T(1,128)S(1)} %bitcast.114), custom_call_target="tpu_custom_call" | custom-call | flops 8589934592 | bytes 4194304 | tf_op jit(solution)/shard_map/pallas_call | solution.py:39
  82.4 2.4 compare_select_fusion.step_ref
  85.1 1.1 reduce-window.14
  86.5 5.0 %reduce-window.16 = f32[8,4,128]{2,0,1:T(8,128)S(1)} reduce-window(f32[8,4,128]{2,0,1:T(8,128)S(1)} %get-tuple-element.26, f32[]{:T(128)} %constant.7.clone.1), window={size=1x1x128 pad=0_0x0_0x0_127}, to_apply=%region_2.3 | reduce-window | flops 520192 | bytes 32772 | tf_op jit(solution)/shard_map/reduce-window.2
  91.6 15.8 %convolution_convert_fusion.1.value_ref = bf16[1024,1024]{1,0:T(8,128)(2,1)S(1)} fusion(bf16[4096,1024]{1,0:T(8,128)(2,1)} %param.15, bf16[256,4096]{1,0:T(8,128)(2,1)} %copy-done.9, bf16[256,4096]{1,0:T(8,128)(2,1)} %copy-done.12, bf16[256,4096]{1,0:T(8,128)(2,1)} %all-gather.7.cloned.1.call-done.a_ref, bf16[256,4096]{1,0:T(8,128)(2,1)} %all-gather.5.cloned.1.call-done.a_ref), kind=kOutput, calls=%fused_computation.8 | convolution fusion | flops 8624537600 | bytes 18874368 | tf_op jit(solution)/shard_map/dot_general | solution.py:210
  107.4 3.4 %collective-permute-start = (bf16[16,1024]{1,0:T(8,128)(2,1)S(1)}, bf16[16,1024]{1,0:T(8,128)(2,1)S(1)}, u32[]{:S(2)}, u32[]{:S(2)}) collective-permute-start(bf16[16,1024]{1,0:T(8,128)(2,1)S(1)} %get-tuple-element.9), channel_id=1, source_target_pairs={{0,8},{8,16},{16,24},{1,9},{9,17},{17,25},{2,10},{10,18},{18,26},{... | collective-permute-start | bytes 98312 | tf_op jit(solution)/shard_map/ppermute | solution.py:160
  110.8 1.5 collective-permute-start.1
  112.4 3.9 %convolution_convert_fusion.2.b_ref.c_ref = bf16[1024,256]{1,0:T(8,128)(2,1)S(1)} fusion(bf16[4096,256]{1,0:T(8,128)(2,1)S(1)} %copy-done, bf16[256,4096]{1,0:T(8,128)(2,1)S(1)} %copy-done.11, bf16[256,4096]{1,0:T(8,128)(2,1)S(1)} %copy-done.13, bf16[256,4096]{1,0:T(8,128)(2,1)S(1)} %copy-done.18, bf16[256,4096]{1,0:T(8,128)(2,1)} %all-gather.5.cloned.1.call-done.a_ref), kind=kOutput, calls=%fused_computation.10 | convolution fusion | flops 2181300224 | bytes 11010048 | tf_op jit(solution)/shard_map/dot_general | solution.py:210
  116.3 0.2 copy.28
  116.6 14.5 %shard_map.129 = (bf16[1024,1024]{1,0:T(8,128)(2,1)}, bf16[2,8,144,128]{3,2,1,0:T(8,128)(2,1)}) custom-call(bf16[1024,1024]{1,0:T(8,128)(2,1)} %copy-done.14, bf16[32,1024]{1,0:T(8,128)(2,1)S(1)} %pad_maximum_fusion.10.halo_ref, f32[4,1024]{1,0:T(4,128)S(1)} %copy-done.3, bf16[1024,256]{1,0:T(8,128)(2,1)S(1)} %convolution_convert_fusion.2.b_ref.c_ref, ...), custom_call_target="tpu_custom_call" | custom-call | tf_op jit(solution)/shard_map/pallas_call | solution.py:235
  131.2 40.5 %shard_map.132 = bf16[1024,4096]{1,0:T(8,128)(2,1)} custom-call(bf16[1024,4096]{1,0:T(8,128)(2,1)} %a_ref.1, s32[1,4096]{1,0:T(1,128)S(1)} %bitcast.115), custom_call_target="tpu_custom_call" | custom-call | flops 34359738368 | bytes 16777216 | tf_op jit(solution)/shard_map/pallas_call | solution.py:39
  171.8 16.8 %convolution_convert_fusion.gate_ref = bf16[1024,1024]{1,0:T(8,128)(2,1)} fusion(bf16[4096,1024]{1,0:T(8,128)(2,1)} %param.14, bf16[256,4096]{1,0:T(8,128)(2,1)} %copy-done.9, bf16[256,4096]{1,0:T(8,128)(2,1)} %copy-done.12, bf16[256,4096]{1,0:T(8,128)(2,1)} %all-gather.7.cloned.1.call-done.a_ref, bf16[256,4096]{1,0:T(8,128)(2,1)} %all-gather.5.cloned.1.call-done.a_ref), kind=kOutput, calls=%fused_computation.7 | convolution fusion | flops 8624537600 | bytes 18874368 | tf_op jit(solution)/shard_map/dot_general | solution.py:210
  188.6 11.9 %shard_map.130.y_ref = f32[1024,1024]{1,0:T(8,128)} custom-call(f32[8]{0:T(128)S(1)} %copy-done.8, bf16[1024,1024]{1,0:T(8,128)(2,1)S(1)} %copy-done.5, bf16[1024,256]{1,0:T(8,128)(2,1)S(1)} %convolution_convert_fusion.2.b_ref.c_ref, bf16[1024,256]{1,0:T(8,128)(2,1)S(1)} %convolution_convert_fusion.2.b_ref.c_ref, f32[1024,8]{1,0:T(8,128)S(1)} %bitcast.109, ...), custom_call_target="tpu_custom_call" | custom-call | flops 2147483648 | bytes 8388608 | tf_op jit(solution)/shard_map/pallas_call | solution.py:259
  200.4 0.9 slice_convert_fusion.1
  201.3 2.1 slice_convert_fusion
  203.5 0.2 fusion.17
  203.7 0.2 fusion.8
  204.1 12.0 %shard_map.131 = bf16[512,2048]{1,0:T(8,128)(2,1)S(1)} custom-call(f32[1024,1024]{1,0:T(8,128)} %shard_map.130.y_ref, bf16[1024,256]{1,0:T(8,128)(2,1)S(1)} %convolution_convert_fusion.2.b_ref.c_ref, f32[1024,8]{1,0:T(8,128)S(1)} %bitcast.110, bf16[1024,1024]{1,0:T(8,128)(2,1)} %convolution_convert_fusion.gate_ref, f32[1,1024]{1,0:T(1,128)S(1)} %bitcast.112, ...), custom_call_target="tpu_custom_call" | custom-call | tf_op jit(solution)/shard_map/pallas_call | solution.py:282
  216.1 1.3 copy-done.2
  217.5 7.9 %fusion.2 = bf16[256,4096]{1,0:T(8,128)(2,1)} fusion(bf16[1024,4096]{1,0:T(8,128)(2,1)} %shard_map.132, bf16[1024,4096]{1,0:T(8,128)(2,1)S(1)} %bitcast.128, bf16[512,2048]{1,0:T(8,128)(2,1)S(1)} %shard_map.131), kind=kOutput, calls=%fused_computation.4 | convolution fusion | flops 4329570304 | bytes 19922944 | tf_op jit(solution)/shard_map/dot_general | solution.py:301
  225.5 9.6 %fusion.3 = bf16[256,4096]{1,0:T(8,128)(2,1)} fusion(bf16[1024,4096]{1,0:T(8,128)(2,1)} %shard_map.132, bf16[1024,4096]{1,0:T(8,128)(2,1)} %a_ref.1, bf16[512,2048]{1,0:T(8,128)(2,1)} %copy-done.2), kind=kOutput, calls=%fused_computation.5 | convolution fusion | flops 4329570304 | bytes 19922944 | tf_op jit(solution)/shard_map/dot_general | solution.py:301
  235.1 32.8 %reduce-scatter.3.cloned.1.call-done = bf16[256,512]{1,0:T(8,128)(2,1)} async-done(((bf16[256,4096]{1,0:T(8,128)(2,1)}), bf16[256,512]{1,0:T(8,128)(2,1)}) %reduce-scatter.3.cloned.1.call-update) | async-done | bytes 262160 | tf_op jit(solution)/shard_map/reduce_scatter | solution.py:302
  267.9 44.7 %reduce-scatter.5.cloned.1.call-done = bf16[256,512]{1,0:T(8,128)(2,1)} async-done(((bf16[256,4096]{1,0:T(8,128)(2,1)}), bf16[256,512]{1,0:T(8,128)(2,1)}) %reduce-scatter.5.cloned.1.call-update) | async-done | bytes 262160 | tf_op jit(solution)/shard_map/reduce_scatter | solution.py:302
  312.6 1.2 multiply_convert_fusion.1
  313.9 0.8 pad_maximum_fusion.9
  (75 shorter events, 1.2 us)
Async XLA Ops:
  6.5 105.8 %copy-start = (bf16[4096,256]{1,0:T(8,128)(2,1)S(1)}, bf16[4096,256]{1,0:T(8,128)(2,1)}, u32[]{:S(2)}) copy-start(bf16[4096,256]{1,0:T(8,128)(2,1)} %param.16) | copy-start | bytes 6291460
  6.5 33.6 %all-gather.7.cloned.1.call-start = ((), (), s32[]{:S(2)}) async-start(), calls=%async_computation.3 | async-start | bytes 2359296 | tf_op jit(solution)/shard_map/all_gather | solution.py:202
  8.6 61.7 %all-gather.5.cloned.1.call-start = ((), (), s32[]{:S(2)}) async-start(), calls=%async_computation.2 | async-start | bytes 2359296 | tf_op jit(solution)/shard_map/all_gather | solution.py:202
  9.3 191.1 %all-gather.9.cloned.1.call-start = ((), (), s32[]{:S(2)}) async-start(), calls=%async_computation.6 | async-start | bytes 2949120 | tf_op jit(solution)/shard_map/all_gather | solution.py:166
  40.2 0.7 copy-start.6
  40.9 29.4 %copy-start.7 = (s32[4096]{0:T(1024)S(1)}, s32[4096]{0:T(1024)}, u32[]{:S(2)}) copy-start(s32[4096]{0:T(1024)} %param.24) | copy-start | bytes 49156
  52.8 1.3 copy-start.9
  54.1 28.3 %copy-start.20 = (bf16[4096,8]{0,1:T(8,128)(2,1)S(1)}, bf16[4096,8]{0,1:T(8,128)(2,1)}, u32[]{:S(2)}) copy-start(bf16[4096,8]{0,1:T(8,128)(2,1)} %param.17) | copy-start | bytes 196612
  54.1 28.3 %copy-start.21 = (f32[8]{0:T(128)S(1)}, f32[8]{0:T(128)}, u32[]{:S(2)}) copy-start(f32[8]{0:T(128)} %param.18) | copy-start | bytes 100
  70.3 12.1 %copy-start.10 = (bf16[256,4096]{1,0:T(8,128)(2,1)S(1)}, bf16[256,4096]{1,0:T(8,128)(2,1)}, u32[]{:S(2)}) copy-start(bf16[256,4096]{1,0:T(8,128)(2,1)} %copy-done.9) | copy-start | bytes 6291460
  70.3 12.1 %copy-start.17 = (bf16[256,4096]{1,0:T(8,128)(2,1)S(1)}, bf16[256,4096]{1,0:T(8,128)(2,1)}, u32[]{:S(2)}) copy-start(bf16[256,4096]{1,0:T(8,128)(2,1)} %all-gather.7.cloned.1.call-done.a_ref) | copy-start | bytes 6291460
  70.3 12.1 %copy-start.19 = (bf16[256,4096]{1,0:T(8,128)(2,1)S(1)}, bf16[256,4096]{1,0:T(8,128)(2,1)}, u32[]{:S(2)}) copy-start(bf16[256,4096]{1,0:T(8,128)(2,1)} %all-gather.5.cloned.1.call-done.a_ref) | copy-start | bytes 6291460
  82.4 2.5 copy-start.12
  82.4 2.6 copy-start.16
  91.5 20.8 %copy-start.11 = (bf16[256,4096]{1,0:T(8,128)(2,1)S(1)}, bf16[256,4096]{1,0:T(8,128)(2,1)}, u32[]{:S(2)}) copy-start(bf16[256,4096]{1,0:T(8,128)(2,1)} %copy-done.9) | copy-start | bytes 6291460
  91.6 20.8 %copy-start.13 = (bf16[256,4096]{1,0:T(8,128)(2,1)S(1)}, bf16[256,4096]{1,0:T(8,128)(2,1)}, u32[]{:S(2)}) copy-start(bf16[256,4096]{1,0:T(8,128)(2,1)} %copy-done.12) | copy-start | bytes 6291460
  91.6 20.8 %copy-start.18 = (bf16[256,4096]{1,0:T(8,128)(2,1)S(1)}, bf16[256,4096]{1,0:T(8,128)(2,1)}, u32[]{:S(2)}) copy-start(bf16[256,4096]{1,0:T(8,128)(2,1)} %all-gather.7.cloned.1.call-done.a_ref) | copy-start | bytes 6291460
  107.4 8.9 %copy-start.14 = (bf16[1024,1024]{1,0:T(8,128)(2,1)}, bf16[1024,1024]{1,0:T(8,128)(2,1)S(1)}, u32[]{:S(2)}) copy-start(bf16[1024,1024]{1,0:T(8,128)(2,1)S(1)} %convolution_convert_fusion.1.value_ref) | copy-start | bytes 6291460
  107.4 9.1 %collective-permute-start = (bf16[16,1024]{1,0:T(8,128)(2,1)S(1)}, bf16[16,1024]{1,0:T(8,128)(2,1)S(1)}, u32[]{:S(2)}, u32[]{:S(2)}) collective-permute-start(bf16[16,1024]{1,0:T(8,128)(2,1)S(1)} %get-tuple-element.9), channel_id=1, source_target_pairs={{0,8},{8,16},{16,24},{1,9},{9,17},{17,25},{2,10},{10,18},{18,26},{... | collective-permute-start | bytes 98312 | tf_op jit(solution)/shard_map/ppermute | solution.py:160
  110.8 5.8 %collective-permute-start.1 = (bf16[16,1024]{1,0:T(8,128)(2,1)S(1)}, bf16[16,1024]{1,0:T(8,128)(2,1)S(1)}, u32[]{:S(2)}, u32[]{:S(2)}) collective-permute-start(bf16[16,1024]{1,0:T(8,128)(2,1)S(1)} %get-tuple-element.10), channel_id=1, source_target_pairs={{8,0},{16,8},{24,16},{9,1},{17,9},{25,17},{10,2},{18,10},{26,18},{... | collective-permute-start | bytes 98312 | tf_op jit(solution)/shard_map/ppermute | solution.py:160
  112.4 4.2 %copy-start.3 = (f32[4,1024]{1,0:T(4,128)S(1)}, f32[4,1024]{1,0:T(4,128)}, u32[]{:S(2)}) copy-start(f32[4,1024]{1,0:T(4,128)} %taps_ref.1) | copy-start | bytes 49156
  131.1 136.8 %reduce-scatter.3.cloned.1.call-start = ((), (), s32[]{:S(2)}) async-start(), calls=%async_computation.4 | async-start | bytes 2359296 | tf_op jit(solution)/shard_map/reduce_scatter | solution.py:302
  171.8 16.8 %copy-start.5 = (bf16[1024,1024]{1,0:T(8,128)(2,1)S(1)}, bf16[1024,1024]{1,0:T(8,128)(2,1)}, u32[]{:S(2)}) copy-start(bf16[1024,1024]{1,0:T(8,128)(2,1)} %get-tuple-element.7.xs_ref) | copy-start | bytes 6291460
  171.8 16.8 %copy-start.8 = (f32[8]{0:T(128)S(1)}, f32[8]{0:T(128)}, u32[]{:S(2)}) copy-start(f32[8]{0:T(128)} %skip_ref.1) | copy-start | bytes 100
  188.6 15.5 %copy-start.4 = (f32[1024]{0:T(1024)S(1)}, f32[1024]{0:T(1024)}, u32[]{:S(2)}) copy-start(f32[1024]{0:T(1024)} %param.22) | copy-start | bytes 12292
  203.5 14.0 %slice-start = ((s8[8388608]{0:T(1024)(128)(4,1)}), s8[4194304]{0:T(1024)(128)(4,1)S(1)}, s32[]{:S(2)}) async-start(s8[8388608]{0:T(1024)(128)(4,1)} %bitcast.127), calls=%async_computation.7 | async-start | bytes 8388608
  204.1 13.4 %slice-start.1 = ((s8[8388608]{0:T(1024)(128)(4,1)}), s8[4194304]{0:T(1024)(128)(4,1)S(1)}, s32[]{:S(2)}) async-start(s8[8388608]{0:T(1024)(128)(4,1)} %bitcast.127), calls=%async_computation.8 | async-start | bytes 8388608
  216.1 1.3 copy-start.2
  225.4 87.3 %copy-start.15 = (s32[512,512]{1,0:T(8,128)S(1)}, s32[512,512]{1,0:T(8,128)}, u32[]{:S(2)}) copy-start(s32[512,512]{1,0:T(8,128)} %param.25) | copy-start | bytes 3145732
  225.4 87.2 %reduce-scatter.5.cloned.1.call-start = ((), (), s32[]{:S(2)}) async-start(), calls=%async_computation.5 | async-start | bytes 2359296 | tf_op jit(solution)/shard_map/reduce_scatter | solution.py:302
  225.4 89.2 %copy-start.1 = (bf16[4096,256]{1,0:T(8,128)(2,1)S(1)}, bf16[4096,256]{1,0:T(8,128)(2,1)}, u32[]{:S(2)}) copy-start(bf16[4096,256]{1,0:T(8,128)(2,1)} %param.16) | copy-start | bytes 6291460
Sparse Core Ops, SparseCore 0:
  9.2 30.8 all-gather.6
  42.0 28.1 all-gather.4
  131.3 51.6 all-gather.8
  225.5 42.3 reduce-scatter.2
  271.4 41.2 reduce-scatter.4

commit v2 on v1

--- a/solution.py
+++ b/solution.py
@@ -10,6 +10,8 @@
 KW = 4
 HALO = 16
 TILE = 256
+DEPTH = 256
+MESH = pl.DeviceIdType.MESH
 F32 = jnp.float32
 BF16 = jnp.bfloat16
 VMEM_LIMIT = 50 * 1024 * 1024
@@ -21,15 +23,19 @@
     )
 
 
+def chosen_rows(partner, low, depth):
+    local = jnp.clip(partner - low, -1, depth).astype(F32).astype(BF16)
+    source = lax.broadcasted_iota(jnp.int32, (depth, partner.shape[1]), 0)
+    source = source.astype(F32).astype(BF16)
+    return jnp.where(source == local, jnp.ones((), BF16), jnp.zeros((), BF16))
+
+
 def permute_body(a_ref, partner_ref, out_ref):
     width = a_ref.shape[1]
-    tile = out_ref.shape[1]
-    depth = min(1024, width)
     total = jnp.zeros(out_ref.shape, F32)
-    for low in range(0, width, depth):
-        source = lax.broadcasted_iota(jnp.int32, (depth, tile), 0) + low
-        chosen = jnp.where(source == partner_ref[...], 1.0, 0.0).astype(BF16)
-        total += jnp.dot(a_ref[:, low : low + depth], chosen, preferred_element_type=F32)
+    for low in range(0, width, DEPTH):
+        chosen = chosen_rows(partner_ref[...], low, DEPTH)
+        total += jnp.dot(a_ref[:, low : low + DEPTH], chosen, preferred_element_type=F32)
     out_ref[...] = total.astype(BF16)
 
 
@@ -160,19 +166,245 @@
     return lax.ppermute(block, "seq", route)
 
 
-def entering(packed, nstate):
+def chain_body(packed_ref, enter_ref, inbox, outbox, send_sem, recv_sem):
+    heads = packed_ref.shape[1]
+    nstate = inbox.shape[2]
     count = lax.axis_size("seq")
     place = lax.axis_index("seq")
-    gathered = lax.all_gather(packed, "seq")
-    ends = gathered[:, :, :, :nstate, :].astype(F32)
-    decays = gathered[:, :, :, nstate : nstate + 1, :].astype(F32)
-    ahead = jnp.zeros(ends.shape[2:], F32)
-    for z in range(count):
-        ahead = jnp.where(z < place, decays[z, 0] * ahead + ends[z, 0], ahead)
-    behind = jnp.zeros(ends.shape[2:], F32)
-    for z in reversed(range(count)):
-        behind = jnp.where(z > place, decays[z, 1] * behind + ends[z, 1], behind)
-    return jnp.stack([ahead, behind]).astype(BF16)
+    toward = [(place + 1) % count, (place + count - 1) % count]
+    first = [place == 0, place == count - 1]
+    last = [place == count - 1, place == 0]
+
+    barrier = pltpu.get_barrier_semaphore()
+    for branch in (0, 1):
+
+        @pl.when(jnp.logical_not(last[branch]))
+        def _(branch=branch):
+            pl.semaphore_signal(
+                barrier, inc=1, device_id={"seq": toward[branch]}, device_id_type=MESH
+            )
+
+    pl.semaphore_wait(barrier, jnp.where(place == 0, 0, 1) + jnp.where(place == count - 1, 0, 1))
+
+    def copy(branch, head):
+        return pltpu.make_async_remote_copy(
+            src_ref=outbox.at[branch, head],
+            dst_ref=inbox.at[branch, head],
+            send_sem=send_sem.at[branch, head],
+            recv_sem=recv_sem.at[branch, head],
+            device_id={"seq": toward[branch]},
+            device_id_type=MESH,
+        )
+
+    def relay(branch, head):
+        copy(branch, head).wait_recv()
+        arrived = inbox[branch, head]
+        enter_ref[branch, head] = arrived
+
+        @pl.when(jnp.logical_not(last[branch]))
+        def _():
+            decay = packed_ref[branch, head, nstate : nstate + 1, :].astype(F32)
+            end = packed_ref[branch, head, :nstate, :].astype(F32)
+            outbox[branch, head] = (decay * arrived.astype(F32) + end).astype(BF16)
+            copy(branch, head).start()
+
+    for branch in (0, 1):
+
+        @pl.when(first[branch])
+        def _(branch=branch):
+            for head in range(heads):
+                enter_ref[branch, head] = jnp.zeros(inbox.shape[2:], BF16)
+                outbox[branch, head] = packed_ref[branch, head, :nstate, :]
+                copy(branch, head).start()
+
+    for head in range(heads):
+        for branch in (0, 1):
+
+            @pl.when(jnp.logical_not(first[branch]))
+            def _(branch=branch, head=head):
+                relay(branch, head)
+
+    for branch in (0, 1):
+
+        @pl.when(jnp.logical_not(last[branch]))
+        def _(branch=branch):
+            for head in range(heads):
+                copy(branch, head).wait_send()
+
+
+def entering(packed, nstate):
+    _, heads, _, head_dim = packed.shape
+    shape = (2, heads, nstate, head_dim)
+    vmem = pl.BlockSpec(memory_space=pltpu.VMEM)
+    return pl.pallas_call(
+        chain_body,
+        in_specs=[vmem],
+        out_specs=vmem,
+        out_shape=jax.ShapeDtypeStruct(shape, BF16),
+        scratch_shapes=[
+            pltpu.VMEM(shape, BF16),
+            pltpu.VMEM(shape, BF16),
+            pltpu.SemaphoreType.DMA((2, heads)),
+            pltpu.SemaphoreType.DMA((2, heads)),
+        ],
+        compiler_params=pltpu.CompilerParams(
+            collective_id=1, has_side_effects=True, vmem_limit_bytes=VMEM_LIMIT
+        ),
+    )(packed)
+
+
+def flip(me, bit):
+    return me + bit * (1 - 2 * ((me // bit) % 2))
+
+
+def greet(partners):
+    barrier = pltpu.get_barrier_semaphore()
+    for partner in partners:
+        pl.semaphore_signal(barrier, inc=1, device_id={"chan": partner}, device_id_type=MESH)
+    pl.semaphore_wait(barrier, len(partners))
+
+
+def output_body(
+    normed_ref, table_ref, partner_ref, out_ref,
+    reverse, total, mine, theirs, sent, diagonal, across,
+    core_send, core_recv, chip_send, chip_recv,
+):
+    rows, width = reverse.shape
+    inner = table_ref.shape[0]
+    cols = out_ref.shape[1]
+    half = rows // 2
+    me = lax.axis_index("chan")
+    mate, beside, above = flip(me, 1), flip(me, 2), flip(me, 4)
+    greet((mate, beside, above))
+
+    def at(block):
+        return pl.ds(pl.multiple_of(block * cols, cols), cols)
+
+    def project(block, carry):
+        reverse[:, at(block)] = jnp.dot(
+            normed_ref[:, inner:], table_ref[:, at(block)], preferred_element_type=F32
+        ).astype(BF16)
+        return carry
+
+    lax.fori_loop(0, width // cols, project, 0)
+
+    def remote(src, dst, send_sem, recv_sem, to):
+        return pltpu.make_async_remote_copy(
+            src_ref=src, dst_ref=dst, send_sem=send_sem, recv_sem=recv_sem,
+            device_id={"chan": to}, device_id_type=MESH,
+        )
+
+    def core_copy(slot):
+        return remote(
+            mine.at[slot], theirs.at[slot], core_send.at[slot], core_recv.at[slot], mate
+        )
+
+    low, high = pl.ds(0, half), pl.ds(half, half)
+    chip_copies = [
+        remote(sent.at[0, low], diagonal.at[0], chip_send.at[0], chip_recv.at[0], beside),
+        remote(sent.at[0, high], diagonal.at[1], chip_send.at[1], chip_recv.at[1], above),
+        remote(sent.at[1, low], across.at[0, low], chip_send.at[2], chip_recv.at[2], beside),
+        remote(sent.at[1, high], across.at[0, high], chip_send.at[3], chip_recv.at[3], beside),
+        remote(sent.at[2, high], across.at[1, high], chip_send.at[4], chip_recv.at[4], above),
+        remote(sent.at[2, low], across.at[1, low], chip_send.at[5], chip_recv.at[5], above),
+    ]
+
+    def stage(chip, carry):
+        is_beside = (chip == 0) | (chip == 1)
+        is_above = (chip == 0) | (chip == 2)
+        base = jnp.where(is_beside, beside - me, 0) + jnp.where(is_above, above - me, 0) + me
+
+        def compute(turn, inner_carry):
+            block = jnp.where(turn == 0, flip(base, 1), base)
+            partner = partner_ref[:, at(block)]
+            part = jnp.dot(
+                normed_ref[:, :inner], table_ref[:, at(block)], preferred_element_type=F32
+            )
+            for depth in range(0, width, DEPTH):
+                part += jnp.dot(
+                    reverse[:, depth : depth + DEPTH],
+                    chosen_rows(partner, depth, DEPTH),
+                    preferred_element_type=F32,
+                )
+            total[...] = part
+
+            @pl.when(turn == 0)
+            def _():
+                mine[chip] = part.astype(BF16)
+                core_copy(chip).start()
+
+            return inner_carry
+
+        lax.fori_loop(0, 2, compute, 0)
+        core_copy(chip).wait_recv()
+        total[...] += theirs[chip].astype(F32)
+
+        @pl.when(chip == 0)
+        def _():
+            sent[0] = total[...].astype(BF16)
+            chip_copies[0].start()
+            chip_copies[1].start()
+
+        @pl.when(chip == 1)
+        def _():
+            sent[1, :half] = total[:half].astype(BF16)
+            chip_copies[2].start()
+            chip_copies[1].wait_recv()
+            sent[1, half:] = (total[half:] + diagonal[1].astype(F32)).astype(BF16)
+            chip_copies[3].start()
+
+        @pl.when(chip == 2)
+        def _():
+            sent[2, half:] = total[half:].astype(BF16)
+            chip_copies[4].start()
+            chip_copies[0].wait_recv()
+            sent[2, :half] = (total[:half] + diagonal[0].astype(F32)).astype(BF16)
+            chip_copies[5].start()
+
+        return carry
+
+    lax.fori_loop(0, 4, stage, 0)
+    for copy in chip_copies[2:]:
+        copy.wait_recv()
+    out_ref[...] = total[...] + across[0].astype(F32) + across[1].astype(F32)
+    for slot in range(4):
+        core_copy(slot).wait_send()
+    for copy in chip_copies:
+        copy.wait_send()
+
+
+def output_sum(normed, table, partner, cols):
+    rows = normed.shape[0]
+    width = table.shape[1]
+    vmem = pl.BlockSpec(memory_space=pltpu.VMEM)
+    block = (rows, cols)
+    return pl.pallas_call(
+        output_body,
+        in_specs=[vmem] * 3,
+        out_specs=vmem,
+        out_shape=jax.ShapeDtypeStruct(block, F32),
+        scratch_shapes=[
+            pltpu.VMEM((rows, width), BF16),
+            pltpu.VMEM(block, F32),
+            pltpu.VMEM((4,) + block, BF16),
+            pltpu.VMEM((4,) + block, BF16),
+            pltpu.VMEM((3,) + block, BF16),
+            pltpu.VMEM((2, rows // 2, cols), BF16),
+            pltpu.VMEM((2,) + block, BF16),
+            pltpu.SemaphoreType.DMA((4,)),
+            pltpu.SemaphoreType.DMA((4,)),
+            pltpu.SemaphoreType.DMA((6,)),
+            pltpu.SemaphoreType.DMA((6,)),
+        ],
+        compiler_params=pltpu.CompilerParams(
+            collective_id=2, has_side_effects=True, vmem_limit_bytes=VMEM_LIMIT
+        ),
+        cost_estimate=pl.CostEstimate(
+            flops=2 * rows * width * (2 * table.shape[0] + width),
+            bytes_accessed=2 * table.size + 2 * normed.size,
+            transcendentals=0,
+        ),
+    )(normed, table, partner)
 
 
 def shards(
@@ -202,7 +434,6 @@
         lax.all_gather(tokens[low : low + half], "chan", axis=1, tiled=True)
         for low in (0, half)
     ]
-    out_perm = permute_columns(out_proj, partner)
     swapped = [permute_columns(part, partner) for part in parts]
     both = jnp.concatenate(parts + swapped, axis=0)
 
@@ -295,16 +526,8 @@
         compiler_params=params(2),
     )(y, bc, cum, gate, norm_gain[None, :], enter)
 
-    table = jnp.concatenate([out_proj, out_perm], axis=0)
-    results = []
-    for low in (0, half):
-        partial = jnp.dot(normed[low : low + half], table, preferred_element_type=F32)
-        summed = lax.psum_scatter(
-            partial.astype(BF16), "chan", scatter_dimension=1, tiled=True
-        ).astype(F32)
-        kept = keep_mask[low : low + half].astype(F32)
-        results.append((summed * kept * (1.0 / 0.9)).astype(BF16))
-    return jnp.concatenate(results, axis=0)
+    summed = output_sum(normed, out_proj, partner, tokens.shape[1])
+    return (summed * keep_mask.astype(F32) * (1.0 / 0.9)).astype(BF16)
 
 
 def solution(mesh):

time: 322 us -> 281 us (0.87)
  waiting for transfers between devices: 125 us -> 47.9 us
  Pallas kernels: 103 us -> 159 us
  matrix products: 56.4 us -> 39.9 us
  other arithmetic: 11.9 us -> 7.38 us
    pallas_call x0 -> x2, Pallas kernels: none -> 98 us  [the longest x1 56.4 us: entering(): pl.pallas_call(chain_body, in_specs=[vmem], out_specs=vmem, out_shape=jax...]
    reduce_scatter x2 -> x0, waiting for transfers between devices: 77.5 us -> none  [shards(): lax.psum_scatter(partial.astype(BF16), 'chan', scatter_dimension=1, tiled...]
    pallas_call x3 -> x2, Pallas kernels: 64.5 us -> 23.7 us  [permute_columns(): pl.pallas_call(permute_body, grid=(width // tile,), in_specs=[pl.BlockSpe...]
    dot_general x2 -> x0, matrix products: 17.5 us -> none  [shards(): partial = jnp.dot(normed[low:low + half], table, preferred_element_type=F32)]
    another operation x7 -> x4, other arithmetic: 6.7 us -> 6.17 us
  transfers between devices with their start and end apart: 7 -> 4, of which waited for: 4 -> 2; matrix products, arithmetic and copies ran while one was open for 10% -> 8% of each run, Pallas kernels for 20% -> 4%
where the time goes in v2:
time: 281 us; the launch traced here: 280 us
  Pallas kernels  159 us (57%)
  waiting for transfers between devices  47.9 us (17%)
  matrix products  39.9 us (14%)
  between operations  13.8 us (5%)
  local copies, waits for them, and re-layouts  7.48 us (3%)
  other arithmetic  7.38 us (3%)
  starting transfers between devices  4.91 us (2%)
    pallas_call x1, Pallas kernels, entering(): pl.pallas_call(chain_body, in_specs=[vmem], out_specs=vmem, out_shape=jax...  56.4 us
    all_gather x2, waiting for transfers between devices, shards(): lax.all_gather(tokens[low:low + half], 'chan', axis=1, tiled=True)  47.2 us
    pallas_call x1, Pallas kernels, output_sum(): pl.pallas_call(output_body, in_specs=[vmem] * 3, out_specs=vmem, out_shap...  41.6 us
    dot_general x4, matrix products, project(): return jnp.dot(both, weights, preferred_element_type=F32)  39.9 us
    pallas_call x2, Pallas kernels, permute_columns(): pl.pallas_call(permute_body, grid=(width // tile,), in_specs=[pl.BlockSpe...  23.7 us
    pallas_call x1, Pallas kernels, shards(): pl.pallas_call(state_body, grid=grid, in_specs=[block, pl.BlockSpec((HALO...  14.4 us
    pallas_call x1, Pallas kernels, shards(): pl.pallas_call(local_body, grid=grid, in_specs=[pl.BlockSpec(memory_space...  11.8 us
    pallas_call x1, Pallas kernels, shards(): pl.pallas_call(norm_body, grid=grid, in_specs=[block, c_block, column, bl...  11.3 us
  transfers between devices with their start and end apart: 4, of which 2 were waited for; matrix products, arithmetic and copies ran while one was open for 8% of the time, Pallas kernels for 4%

profile of v2, /device:TPU:0, one launch (start us, length us, event | category | flops | bytes accessed | tf_op | source)
XLA Modules:
  0.0 280.4 jit_solution(11435179749913267082)
XLA Ops:
  6.5 2.0 fusion.2
  8.5 0.0 all-gather.5.cloned.1.call-update
  8.6 0.0 all-gather.3.cloned.1.call-start
  8.6 0.7 all-gather.3.cloned.1.call-update
  9.3 30.8 %all-gather.5.cloned.1.call-done.a_ref = bf16[256,4096]{1,0:T(8,128)(2,1)} async-done(((bf16[256,512]{1,0:T(8,128)(2,1)}), bf16[256,4096]{1,0:T(8,128)(2,1)}) %all-gather.5.cloned.1.call-update) | async-done | bytes 2097168 | tf_op jit(solution)/shard_map/all_gather | solution.py:434
  40.2 0.7 copy-done.6
  40.9 11.8 %shard_map.128 = bf16[256,4096]{1,0:T(8,128)(2,1)S(1)} custom-call(bf16[256,4096]{1,0:T(8,128)(2,1)} %all-gather.5.cloned.1.call-done.a_ref, s32[1,4096]{1,0:T(1,128)S(1)} %bitcast.40), custom_call_target="tpu_custom_call" | custom-call | flops 8589934592 | bytes 4194304 | tf_op jit(solution)/shard_map/pallas_call | solution.py:45
  52.7 1.4 copy-done.9
  54.0 16.3 %all-gather.3.cloned.1.call-done.a_ref = bf16[256,4096]{1,0:T(8,128)(2,1)} async-done(((bf16[256,512]{1,0:T(8,128)(2,1)}), bf16[256,4096]{1,0:T(8,128)(2,1)}) %all-gather.3.cloned.1.call-update) | async-done | bytes 2097168 | tf_op jit(solution)/shard_map/all_gather | solution.py:434
  70.4 11.9 %shard_map.127 = bf16[256,4096]{1,0:T(8,128)(2,1)S(1)} custom-call(bf16[256,4096]{1,0:T(8,128)(2,1)} %all-gather.3.cloned.1.call-done.a_ref, s32[1,4096]{1,0:T(1,128)S(1)} %bitcast.41), custom_call_target="tpu_custom_call" | custom-call | flops 8589934592 | bytes 4194304 | tf_op jit(solution)/shard_map/pallas_call | solution.py:45
  82.4 2.4 compare_select_fusion.step_ref
  84.8 0.2 copy.23
  85.0 0.1 negate_multiply_fusion
  85.1 1.1 reduce-window.14
  86.2 0.2 slice_reduce_fusion.1
  86.4 5.0 %reduce-window.16 = f32[8,4,128]{2,0,1:T(8,128)S(1)} reduce-window(f32[8,4,128]{2,0,1:T(8,128)S(1)} %get-tuple-element.16, f32[]{:T(128)} %constant.8.clone.1), window={size=1x1x128 pad=0_0x0_0x0_127}, to_apply=%region_2.3 | reduce-window | flops 520192 | bytes 32772 | tf_op jit(solution)/shard_map/reduce-window.2
  91.4 0.1 slice_reduce_fusion
  91.5 15.8 %convolution_convert_fusion.1.value_ref = bf16[1024,1024]{1,0:T(8,128)(2,1)S(1)} fusion(bf16[4096,1024]{1,0:T(8,128)(2,1)} %param.15, bf16[256,4096]{1,0:T(8,128)(2,1)} %copy-done.9, bf16[256,4096]{1,0:T(8,128)(2,1)} %copy-done.12, bf16[256,4096]{1,0:T(8,128)(2,1)} %all-gather.5.cloned.1.call-done.a_ref, bf16[256,4096]{1,0:T(8,128)(2,1)} %all-gather.3.cloned.1.call-done.a_ref), kind=kOutput, calls=%fused_computation.2 | convolution fusion | flops 8624537600 | bytes 18874368 | tf_op jit(solution)/shard_map/dot_general | solution.py:441
  107.4 3.4 %collective-permute-start = (bf16[16,1024]{1,0:T(8,128)(2,1)S(1)}, bf16[16,1024]{1,0:T(8,128)(2,1)S(1)}, u32[]{:S(2)}, u32[]{:S(2)}) collective-permute-start(bf16[16,1024]{1,0:T(8,128)(2,1)S(1)} %get-tuple-element.9), channel_id=1, source_target_pairs={{0,8},{8,16},{16,24},{1,9},{9,17},{17,25},{2,10},{10,18},{18,26},{... | collective-permute-start | bytes 98312 | tf_op jit(solution)/shard_map/ppermute | solution.py:166
  110.8 1.5 collective-permute-start.1
  112.3 0.1 add_bitcast_fusion
  112.4 3.9 %convolution_convert_fusion.2.b_ref.c_ref = bf16[1024,256]{1,0:T(8,128)(2,1)S(1)} fusion(bf16[4096,256]{1,0:T(8,128)(2,1)S(1)} %copy-done, bf16[256,4096]{1,0:T(8,128)(2,1)S(1)} %copy-done.11, bf16[256,4096]{1,0:T(8,128)(2,1)S(1)} %copy-done.13, bf16[256,4096]{1,0:T(8,128)(2,1)S(1)} %copy-done.18, bf16[256,4096]{1,0:T(8,128)(2,1)} %all-gather.3.cloned.1.call-done.a_ref), kind=kOutput, calls=%fused_computation.4 | convolution fusion | flops 2181300224 | bytes 11010048 | tf_op jit(solution)/shard_map/dot_general | solution.py:441
  116.3 17.7 %convolution_convert_fusion.gate_ref = bf16[1024,1024]{1,0:T(8,128)(2,1)} fusion(bf16[4096,1024]{1,0:T(8,128)(2,1)} %param.14, bf16[256,4096]{1,0:T(8,128)(2,1)S(1)} %copy-done.11, bf16[256,4096]{1,0:T(8,128)(2,1)S(1)} %copy-done.13, bf16[256,4096]{1,0:T(8,128)(2,1)S(1)} %copy-done.18, bf16[256,4096]{1,0:T(8,128)(2,1)} %all-gather.3.cloned.1.call-done.a_ref), kind=kOutput, calls=%fused_computation.1 | convolution fusion | flops 8624537600 | bytes 18874368 | tf_op jit(solution)/shard_map/dot_general | solution.py:441
  134.1 0.2 copy.24
  134.4 1.0 copy-done.2
  135.4 14.4 %shard_map.129 = (bf16[1024,1024]{1,0:T(8,128)(2,1)}, bf16[2,8,144,128]{3,2,1,0:T(8,128)(2,1)S(1)}) custom-call(bf16[1024,1024]{1,0:T(8,128)(2,1)} %copy-done.14, bf16[32,1024]{1,0:T(8,128)(2,1)S(1)} %pad_maximum_fusion.1.halo_ref, f32[4,1024]{1,0:T(4,128)S(1)} %copy-done.3, bf16[1024,256]{1,0:T(8,128)(2,1)S(1)} %convolution_convert_fusion.2.b_ref.c_ref, ...), custom_call_target="tpu_custom_call" | custom-call | tf_op jit(solution)/shard_map/pallas_call | solution.py:466
  149.8 56.4 %shard_map.131.enter_ref = bf16[2,8,128,128]{3,2,1,0:T(8,128)(2,1)S(1)} custom-call(bf16[2,8,144,128]{3,2,1,0:T(8,128)(2,1)S(1)} %get-tuple-element.8.packed_ref), custom_call_target="tpu_custom_call" | custom-call | tf_op jit(solution)/shard_map/pallas_call | solution.py:239
  206.3 1.6 copy-done.5
  207.9 11.8 %shard_map.130.y_ref = f32[1024,1024]{1,0:T(8,128)} custom-call(f32[8]{0:T(128)S(1)} %copy-done.8, bf16[1024,1024]{1,0:T(8,128)(2,1)S(1)} %copy-done.5, bf16[1024,256]{1,0:T(8,128)(2,1)S(1)} %convolution_convert_fusion.2.b_ref.c_ref, bf16[1024,256]{1,0:T(8,128)(2,1)S(1)} %convolution_convert_fusion.2.b_ref.c_ref, f32[1024,8]{1,0:T(8,128)S(1)} %bitcast.36, ...), custom_call_target="tpu_custom_call" | custom-call | flops 2147483648 | bytes 8388608 | tf_op jit(solution)/shard_map/pallas_call | solution.py:490
  219.6 11.3 %shard_map.132.normed_ref = bf16[512,2048]{1,0:T(8,128)(2,1)S(1)} custom-call(f32[1024,1024]{1,0:T(8,128)} %shard_map.130.y_ref, bf16[1024,256]{1,0:T(8,128)(2,1)S(1)} %convolution_convert_fusion.2.b_ref.c_ref, f32[1024,8]{1,0:T(8,128)S(1)} %bitcast.37, bf16[1024,1024]{1,0:T(8,128)(2,1)} %convolution_convert_fusion.gate_ref, f32[1,1024]{1,0:T(1,128)S(1)} %bitcast.39, ...), custom_call_target="tpu_custom_call" | custom-call | tf_op jit(solution)/shard_map/pallas_call | solution.py:513
  231.0 41.6 %shard_map.133 = f32[512,512]{1,0:T(8,128)S(1)} custom-call(bf16[512,2048]{1,0:T(8,128)(2,1)S(1)} %shard_map.132.normed_ref, bf16[1024,4096]{1,0:T(8,128)(2,1)} %table_ref.1, s32[1,4096]{1,0:T(1,128)S(1)} %bitcast.42), custom_call_target="tpu_custom_call" | custom-call | flops 25769803776 | bytes 10485760 | tf_op jit(solution)/shard_map/pallas_call | solution.py:381
  272.5 1.0 multiply_convert_fusion
  (53 shorter events, 0.3 us)
Async XLA Ops:
  6.5 105.8 %copy-start = (bf16[4096,256]{1,0:T(8,128)(2,1)S(1)}, bf16[4096,256]{1,0:T(8,128)(2,1)}, u32[]{:S(2)}) copy-start(bf16[4096,256]{1,0:T(8,128)(2,1)} %param.16) | copy-start | bytes 6291460
  6.5 33.6 %all-gather.5.cloned.1.call-start = ((), (), s32[]{:S(2)}) async-start(), calls=%async_computation.1 | async-start | bytes 2359296 | tf_op jit(solution)/shard_map/all_gather | solution.py:434
  8.6 61.8 %all-gather.3.cloned.1.call-start = ((), (), s32[]{:S(2)}) async-start(), calls=%async_computation | async-start | bytes 2359296 | tf_op jit(solution)/shard_map/all_gather | solution.py:434
  40.2 0.7 copy-start.6
  40.9 29.5 %copy-start.7 = (s32[4096]{0:T(1024)S(1)}, s32[4096]{0:T(1024)}, u32[]{:S(2)}) copy-start(s32[4096]{0:T(1024)} %param.24) | copy-start | bytes 49156
  52.7 1.4 copy-start.9
  54.0 28.3 %copy-start.20 = (bf16[4096,8]{0,1:T(8,128)(2,1)S(1)}, bf16[4096,8]{0,1:T(8,128)(2,1)}, u32[]{:S(2)}) copy-start(bf16[4096,8]{0,1:T(8,128)(2,1)} %param.17) | copy-start | bytes 196612
  54.0 28.3 %copy-start.21 = (f32[8]{0:T(128)S(1)}, f32[8]{0:T(128)}, u32[]{:S(2)}) copy-start(f32[8]{0:T(128)} %param.18) | copy-start | bytes 100
  70.4 12.0 %copy-start.10 = (bf16[256,4096]{1,0:T(8,128)(2,1)S(1)}, bf16[256,4096]{1,0:T(8,128)(2,1)}, u32[]{:S(2)}) copy-start(bf16[256,4096]{1,0:T(8,128)(2,1)} %copy-done.9) | copy-start | bytes 6291460
  70.4 12.0 %copy-start.17 = (bf16[256,4096]{1,0:T(8,128)(2,1)S(1)}, bf16[256,4096]{1,0:T(8,128)(2,1)}, u32[]{:S(2)}) copy-start(bf16[256,4096]{1,0:T(8,128)(2,1)} %all-gather.5.cloned.1.call-done.a_ref) | copy-start | bytes 6291460
  70.4 12.0 %copy-start.19 = (bf16[256,4096]{1,0:T(8,128)(2,1)S(1)}, bf16[256,4096]{1,0:T(8,128)(2,1)}, u32[]{:S(2)}) copy-start(bf16[256,4096]{1,0:T(8,128)(2,1)} %all-gather.3.cloned.1.call-done.a_ref) | copy-start | bytes 6291460
  82.4 2.5 copy-start.12
  82.4 2.6 copy-start.16
  84.8 22.5 %copy-start.1 = (f32[1024,8]{1,0:T(8,128)}, f32[1024,8]{1,0:T(8,128)S(1)}, u32[]{:S(2)}) copy-start(f32[1024,8]{1,0:T(8,128)S(1)} %compare_select_fusion.step_ref) | copy-start | bytes 98308
  91.5 20.8 %copy-start.11 = (bf16[256,4096]{1,0:T(8,128)(2,1)S(1)}, bf16[256,4096]{1,0:T(8,128)(2,1)}, u32[]{:S(2)}) copy-start(bf16[256,4096]{1,0:T(8,128)(2,1)} %copy-done.9) | copy-start | bytes 6291460
  91.5 20.8 %copy-start.13 = (bf16[256,4096]{1,0:T(8,128)(2,1)S(1)}, bf16[256,4096]{1,0:T(8,128)(2,1)}, u32[]{:S(2)}) copy-start(bf16[256,4096]{1,0:T(8,128)(2,1)} %copy-done.12) | copy-start | bytes 6291460
  91.5 20.8 %copy-start.18 = (bf16[256,4096]{1,0:T(8,128)(2,1)S(1)}, bf16[256,4096]{1,0:T(8,128)(2,1)}, u32[]{:S(2)}) copy-start(bf16[256,4096]{1,0:T(8,128)(2,1)} %all-gather.5.cloned.1.call-done.a_ref) | copy-start | bytes 6291460
  107.4 8.9 %copy-start.14 = (bf16[1024,1024]{1,0:T(8,128)(2,1)}, bf16[1024,1024]{1,0:T(8,128)(2,1)S(1)}, u32[]{:S(2)}) copy-start(bf16[1024,1024]{1,0:T(8,128)(2,1)S(1)} %convolution_convert_fusion.1.value_ref) | copy-start | bytes 6291460
  107.4 27.0 %collective-permute-start = (bf16[16,1024]{1,0:T(8,128)(2,1)S(1)}, bf16[16,1024]{1,0:T(8,128)(2,1)S(1)}, u32[]{:S(2)}, u32[]{:S(2)}) collective-permute-start(bf16[16,1024]{1,0:T(8,128)(2,1)S(1)} %get-tuple-element.9), channel_id=1, source_target_pairs={{0,8},{8,16},{16,24},{1,9},{9,17},{17,25},{2,10},{10,18},{18,26},{... | collective-permute-start | bytes 98312 | tf_op jit(solution)/shard_map/ppermute | solution.py:166
  110.8 23.6 %collective-permute-start.1 = (bf16[16,1024]{1,0:T(8,128)(2,1)S(1)}, bf16[16,1024]{1,0:T(8,128)(2,1)S(1)}, u32[]{:S(2)}, u32[]{:S(2)}) collective-permute-start(bf16[16,1024]{1,0:T(8,128)(2,1)S(1)} %get-tuple-element.10), channel_id=1, source_target_pairs={{8,0},{16,8},{24,16},{9,1},{17,9},{25,17},{10,2},{18,10},{26,18},{... | collective-permute-start | bytes 98312 | tf_op jit(solution)/shard_map/ppermute | solution.py:166
  116.3 18.1 %copy-start.3 = (f32[4,1024]{1,0:T(4,128)S(1)}, f32[4,1024]{1,0:T(4,128)}, u32[]{:S(2)}) copy-start(f32[4,1024]{1,0:T(4,128)} %taps_ref.1) | copy-start | bytes 49156
  116.3 89.9 %copy-start.8 = (f32[8]{0:T(128)S(1)}, f32[8]{0:T(128)}, u32[]{:S(2)}) copy-start(f32[8]{0:T(128)} %skip_ref.1) | copy-start | bytes 100
  134.0 85.6 %copy-start.4 = (f32[1024]{0:T(1024)S(1)}, f32[1024]{0:T(1024)}, u32[]{:S(2)}) copy-start(f32[1024]{0:T(1024)} %param.22) | copy-start | bytes 12292
  134.4 1.0 copy-start.2
  206.3 1.6 copy-start.5
  230.9 41.6 %copy-start.15 = (s32[512,512]{1,0:T(8,128)S(1)}, s32[512,512]{1,0:T(8,128)}, u32[]{:S(2)}) copy-start(s32[512,512]{1,0:T(8,128)} %param.25) | copy-start | bytes 3145732
Sparse Core Ops, SparseCore 0:
  9.2 30.8 all-gather.4
  42.0 28.2 all-gather.2

commit v3 on v2

--- a/solution.py
+++ b/solution.py
@@ -30,32 +30,143 @@
     return jnp.where(source == local, jnp.ones((), BF16), jnp.zeros((), BF16))
 
 
-def permute_body(a_ref, partner_ref, out_ref):
-    width = a_ref.shape[1]
-    total = jnp.zeros(out_ref.shape, F32)
-    for low in range(0, width, DEPTH):
-        chosen = chosen_rows(partner_ref[...], low, DEPTH)
-        total += jnp.dot(a_ref[:, low : low + DEPTH], chosen, preferred_element_type=F32)
-    out_ref[...] = total.astype(BF16)
-
-
-def permute_columns(a, partner):
-    rows, width = a.shape
-    tile = 512
+def gather_body(tokens_ref, partner_ref, out_ref, send_sem, recv_sem):
+    rows, cols = tokens_ref.shape
+    width = out_ref.shape[1]
+    half = rows // 2
+    me = lax.axis_index("chan")
+    mate, beside, above = flip(me, 1), flip(me, 2), flip(me, 4)
+    opposite = flip(beside, 4)
+    greet((mate, beside, above))
+    every, low, high = pl.ds(0, rows), pl.ds(0, half), pl.ds(half, half)
+
+    def at(block):
+        return pl.ds(pl.multiple_of(block * cols, cols), cols)
+
+    out_ref[:rows, at(me)] = tokens_ref[...]
+
+    def remote(index, part, owner, to):
+        piece = out_ref.at[part, at(owner)]
+        return pltpu.make_async_remote_copy(
+            src_ref=piece, dst_ref=piece,
+            send_sem=send_sem.at[index], recv_sem=recv_sem.at[index],
+            device_id={"chan": to}, device_id_type=MESH,
+        )
+
+    copies = [
+        remote(0, every, me, mate),
+        remote(1, low, me, beside),
+        remote(2, high, me, beside),
+        remote(3, high, me, above),
+        remote(4, low, me, above),
+        remote(5, low, beside, above),
+        remote(6, high, above, beside),
+        remote(7, every, beside, mate),
+        remote(8, every, above, mate),
+        remote(9, low, opposite, mate),
+        remote(10, high, opposite, mate),
+    ]
+
+    def permute(block, initial):
+        def tile(column, carry):
+            partner = partner_ref[:, at(column)]
+            part = jnp.zeros((rows, cols), F32)
+            for owner in (block, flip(block, 1)):
+                for depth in range(0, cols, DEPTH):
+                    start = pl.multiple_of(owner * cols + depth, DEPTH)
+                    part += jnp.dot(
+                        out_ref[:rows, pl.ds(start, DEPTH)],
+                        chosen_rows(partner, start, DEPTH),
+                        preferred_element_type=F32,
+                    )
+            if not initial:
+                part += out_ref[rows:, at(column)].astype(F32)
+            out_ref[rows:, at(column)] = part.astype(BF16)
+            return carry
+
+        lax.fori_loop(0, width // cols, tile, 0)
+
+    for index in (1, 3, 0, 2, 4):
+        copies[index].start()
+    copies[0].wait_recv()
+    permute(me, True)
+    for arrived, onward in ((1, 5), (3, 6), (2, 7), (4, 8)):
+        copies[arrived].wait_recv()
+        copies[onward].start()
+    copies[7].wait_recv()
+    permute(beside, False)
+    for arrived, onward in ((5, 9), (6, 10)):
+        copies[arrived].wait_recv()
+        copies[onward].start()
+    copies[8].wait_recv()
+    permute(above, False)
+    copies[9].wait_recv()
+    copies[10].wait_recv()
+    permute(opposite, False)
+    for copy in copies:
+        copy.wait_send()
+
+
+def gather_both(tokens, partner):
+    rows, width = tokens.shape[0], partner.shape[1]
+    vmem = pl.BlockSpec(memory_space=pltpu.VMEM)
     return pl.pallas_call(
-        permute_body,
-        grid=(width // tile,),
-        in_specs=[
-            pl.BlockSpec((rows, width), lambda j: (0, 0)),
-            pl.BlockSpec((1, tile), lambda j: (0, j)),
-        ],
-        out_specs=pl.BlockSpec((rows, tile), lambda j: (0, j)),
-        out_shape=jax.ShapeDtypeStruct((rows, width), BF16),
+        gather_body,
+        in_specs=[vmem] * 2,
+        out_specs=vmem,
+        out_shape=jax.ShapeDtypeStruct((2 * rows, width), BF16),
+        scratch_shapes=[pltpu.SemaphoreType.DMA((11,)), pltpu.SemaphoreType.DMA((11,))],
+        compiler_params=pltpu.CompilerParams(
+            collective_id=3, has_side_effects=True, vmem_limit_bytes=VMEM_LIMIT
+        ),
+        cost_estimate=pl.CostEstimate(
+            flops=2 * rows * width * width, bytes_accessed=6 * rows * width, transcendentals=0
+        ),
+    )(tokens, partner)
+
+
+def product_body(counts, a_ref, *refs):
+    step = pl.program_id(0)
+    begin = 0
+    for index, count in enumerate(counts):
+        weight_ref, out_ref = refs[index], refs[len(counts) + index]
+
+        @pl.when((step >= begin) & (step < begin + count))
+        def _(weight_ref=weight_ref, out_ref=out_ref):
+            out_ref[...] = jnp.dot(
+                a_ref[...], weight_ref[...], preferred_element_type=F32
+            ).astype(BF16)
+
+        begin += count
+
+
+def products(a, weights):
+    rows, depth = a.shape
+    counts = tuple(w.shape[1] // TILE for w in weights)
+    steps = sum(counts)
+
+    def tile_of(index):
+        begin = sum(counts[:index])
+        return lambda j: (0, jnp.clip(j - begin, 0, counts[index] - 1))
+
+    return pl.pallas_call(
+        functools.partial(product_body, counts),
+        grid=(steps,),
+        in_specs=[pl.BlockSpec((rows, depth), lambda j: (0, 0))]
+        + [pl.BlockSpec((depth, TILE), tile_of(i)) for i in range(len(weights))],
+        out_specs=[pl.BlockSpec((rows, TILE), tile_of(i)) for i in range(len(weights))],
+        out_shape=[jax.ShapeDtypeStruct((rows, w.shape[1]), BF16) for w in weights],
         compiler_params=params(1),
         cost_estimate=pl.CostEstimate(
-            flops=2 * rows * width * width, bytes_accessed=4 * rows * width, transcendentals=0
-        ),
-    )(a, partner)
+            flops=2 * rows * depth * TILE * steps,
+            bytes_accessed=2 * (rows * depth + (depth + rows) * TILE * steps),
+            transcendentals=0,
+        ),
+    )(a, *weights)
+
+
+def silu(v):
+    return 0.5 * v * (1.0 + jnp.tanh(0.5 * v))
 
 
 def column_of(ref, head):
@@ -74,7 +185,7 @@
     cum = column_of(cum_ref, head)
 
     def finish(conv, end):
-        xs = (conv / (1.0 + jnp.exp(-conv))).astype(BF16)
+        xs = silu(conv).astype(BF16)
         xs_ref[...] = xs
         weighted = (xs.astype(F32) * (jnp.exp(end - cum) * step)).astype(BF16)
         state = lax.dot_general(
@@ -155,7 +266,7 @@
     carried = jnp.dot(c_ref[...], enter_ref[0, 0], preferred_element_type=F32)
     y = y_ref[...] + jnp.exp(cum) * carried
     gate = gate_ref[...].astype(F32)
-    gated = y * (gate / (1.0 + jnp.exp(-gate)))
+    gated = y * silu(gate)
     mean = jnp.mean(gated * gated, axis=1, keepdims=True)
     out_ref[...] = (gated * lax.rsqrt(mean + 1e-05) * gain_ref[...]).astype(BF16)
 
@@ -217,12 +328,13 @@
                 outbox[branch, head] = packed_ref[branch, head, :nstate, :]
                 copy(branch, head).start()
 
-    for head in range(heads):
-        for branch in (0, 1):
-
-            @pl.when(jnp.logical_not(first[branch]))
-            def _(branch=branch, head=head):
-                relay(branch, head)
+    for near, order in ((2 * place < count, (0, 1)), (2 * place >= count, (1, 0))):
+        for branch in order:
+
+            @pl.when(near & jnp.logical_not(first[branch]))
+            def _(branch=branch):
+                for head in range(heads):
+                    relay(branch, head)
 
     for branch in (0, 1):
 
@@ -428,24 +540,14 @@
     head_dim = inner // heads
     nstate = state_proj.shape[1] // 2
     partner = complement[None, :]
-    half = rows // 2
-
-    parts = [
-        lax.all_gather(tokens[low : low + half], "chan", axis=1, tiled=True)
-        for low in (0, half)
-    ]
-    swapped = [permute_columns(part, partner) for part in parts]
-    both = jnp.concatenate(parts + swapped, axis=0)
-
-    def project(weights):
-        return jnp.dot(both, weights, preferred_element_type=F32)
-
-    value = project(value_proj).astype(BF16)
+
+    both = gather_both(tokens, partner)
+    value, bc = products(both, (value_proj, state_proj))
     halo = jnp.concatenate(
         [shift(value[rows - HALO : rows], 1), shift(value[rows : rows + HALO], -1)], axis=0
     )
-    bc = project(state_proj).astype(BF16)
-    step = jax.nn.softplus(project(step_proj) + step_bias).reshape(2, rows, heads)
+    step_raw = jnp.dot(both, step_proj, preferred_element_type=F32)
+    step = jax.nn.softplus(step_raw + step_bias).reshape(2, rows, heads)
     log_decay = -step * decay_rate
     cum = jnp.stack(
         [jnp.cumsum(log_decay[0], axis=0), lax.cumsum(log_decay[1], axis=0, reverse=True)]
@@ -454,7 +556,7 @@
     cum_rows = jnp.swapaxes(cum, 1, 2).reshape(2 * heads, 1, rows)
     step = step.reshape(2 * rows, heads)
     cum = cum.reshape(2 * rows, heads)
-    gate = project(gate_proj).astype(BF16)
+    (gate,) = products(both, (gate_proj,))
 
     grid = (2, heads)
     block = pl.BlockSpec((rows, head_dim), lambda b, h: (b, h))

time: 281 us -> 189 us (0.67)
  waiting for transfers between devices: 47.9 us -> 0.01 us
  matrix products: 39.9 us -> 2.42 us
  between operations: 13.8 us -> 0.29 us
  Pallas kernels: 159 us -> 166 us
    all_gather x2 -> x0, waiting for transfers between devices: 47.2 us -> none  [shards(): lax.all_gather(tokens[low:low + half], 'chan', axis=1, tiled=True)]
    pallas_call x2 -> x3, Pallas kernels: 23.7 us -> 68.6 us  [the longest x1 38 us: gather_both(): pl.pallas_call(gather_body, in_specs=[vmem] * 2, out_specs=vmem, out_shap...]
    pallas_call x1, Pallas kernels: 56.4 us -> 18.7 us  [entering(): pl.pallas_call(chain_body, in_specs=[vmem], out_specs=vmem, out_shape=jax...]
    dot_general x4 -> x1, matrix products: 39.9 us -> 2.42 us  [shards(): step_raw = jnp.dot(both, step_proj, preferred_element_type=F32)]
    unnamed x44 -> x32, local copies, waits for them, and re-layouts: 4.77 us -> 5.77 us
  transfers between devices with their start and end apart: 4 -> 2, of which waited for: 2 -> 0; matrix products, arithmetic and copies ran while one was open for 8% -> 5% of each run, Pallas kernels for 4% -> 7%
where the time goes in v3:
time: 189 us; the launch traced here: 188 us
  Pallas kernels  166 us (88%)
  other arithmetic  7.38 us (4%)
  local copies, waits for them, and re-layouts  6.48 us (3%)
  starting transfers between devices  5.1 us (3%)
  matrix products  2.42 us (1%)
    pallas_call x1, Pallas kernels, output_sum(): pl.pallas_call(output_body, in_specs=[vmem] * 3, out_specs=vmem, out_shap...  41.9 us
    pallas_call x1, Pallas kernels, gather_both(): pl.pallas_call(gather_body, in_specs=[vmem] * 2, out_specs=vmem, out_shap...  38 us
    pallas_call x2, Pallas kernels, products(): pl.pallas_call(functools.partial(product_body, counts), grid=(steps,), in...  30.6 us
    pallas_call x1, Pallas kernels, entering(): pl.pallas_call(chain_body, in_specs=[vmem], out_specs=vmem, out_shape=jax...  18.7 us
    pallas_call x1, Pallas kernels, shards(): pl.pallas_call(state_body, grid=grid, in_specs=[block, pl.BlockSpec((HALO...  14.2 us
    pallas_call x1, Pallas kernels, shards(): pl.pallas_call(local_body, grid=grid, in_specs=[pl.BlockSpec(memory_space...  11.7 us
    pallas_call x1, Pallas kernels, shards(): pl.pallas_call(norm_body, grid=grid, in_specs=[block, c_block, column, bl...  11.2 us
    another operation x4, other arithmetic  6.17 us
  transfers between devices with their start and end apart: 2, of which 0 were waited for; matrix products, arithmetic and copies ran while one was open for 5% of the time, Pallas kernels for 7%

profile of v3, /device:TPU:0, one launch (start us, length us, event | category | flops | bytes accessed | tf_op | source)
XLA Modules:
  0.0 188.1 jit_solution(2924266979996234318)
XLA Ops:
  0.0 1.1 copy-done.8
  1.1 0.7 copy-done.9
  1.8 38.0 %shard_map.127.a_ref = bf16[1024,4096]{1,0:T(8,128)(2,1)} custom-call(bf16[512,512]{1,0:T(8,128)(2,1)S(1)} %copy-done.8, s32[1,4096]{1,0:T(1,128)S(1)} %bitcast.38), custom_call_target="tpu_custom_call" | custom-call | flops 17179869184 | bytes 12582912 | tf_op jit(solution)/shard_map/pallas_call | solution.py:113
  39.8 0.0 copy-start.14
  39.9 16.9 %shard_map.128 = (bf16[1024,1024]{1,0:T(8,128)(2,1)S(1)}, bf16[1024,256]{1,0:T(8,128)(2,1)S(1)}) custom-call(bf16[1024,4096]{1,0:T(8,128)(2,1)} %shard_map.127.a_ref, bf16[4096,1024]{1,0:T(8,128)(2,1)} %refs_0_.2, bf16[4096,256]{1,0:T(8,128)(2,1)} %refs_1_.1), custom_call_target="tpu_custom_call" | custom-call | flops 10737418240 | bytes 21495808 | tf_op jit(solution)/shard_map/pallas_call | solution.py:152
  56.8 0.0 copy-start.13
  56.8 3.6 %collective-permute-start = (bf16[16,1024]{1,0:T(8,128)(2,1)S(1)}, bf16[16,1024]{1,0:T(8,128)(2,1)S(1)}, u32[]{:S(2)}, u32[]{:S(2)}) collective-permute-start(bf16[16,1024]{1,0:T(8,128)(2,1)S(1)} %get-tuple-element.13), channel_id=1, source_target_pairs={{0,8},{8,16},{16,24},{1,9},{9,17},{17,25},{2,10},{10,18},{18,26},{... | collective-permute-start | bytes 98312 | tf_op jit(solution)/shard_map/ppermute | solution.py:277
  60.4 1.5 collective-permute-start.1
  61.9 2.4 %compare_select_fusion.step_ref = f32[1024,8]{1,0:T(8,128)S(1)} fusion(bf16[1024,4096]{1,0:T(8,128)(2,1)S(1)} %copy-done.15, bf16[4096,8]{0,1:T(8,128)(2,1)S(1)} %copy-done, f32[8]{0:T(128)S(1)} %copy-done.14), kind=kOutput, calls=%fused_computation | convolution fusion | flops 67166208 | bytes 8486944 | tf_op jit(solution)/shard_map/dot_general | solution.py:549
  64.4 0.0 copy-start.2
  64.4 0.2 copy.23
  64.5 0.1 negate_multiply_fusion
  64.6 1.1 reduce-window.14
  65.8 0.2 slice_reduce_fusion.1
  66.0 5.0 %reduce-window.16 = f32[8,4,128]{2,0,1:T(8,128)S(1)} reduce-window(f32[8,4,128]{2,0,1:T(8,128)S(1)} %get-tuple-element.18, f32[]{:T(128)} %constant.8.clone.1), window={size=1x1x128 pad=0_0x0_0x0_127}, to_apply=%region_2.3 | reduce-window | flops 520192 | bytes 32772 | tf_op jit(solution)/shard_map/reduce-window.2
  70.9 0.1 slice_reduce_fusion
  71.1 0.0 copy-start.11
  71.1 13.7 %shard_map.131.gate_ref = bf16[1024,1024]{1,0:T(8,128)(2,1)S(1)} custom-call(bf16[1024,4096]{1,0:T(8,128)(2,1)} %shard_map.127.a_ref, bf16[4096,1024]{1,0:T(8,128)(2,1)} %refs_0_.3), custom_call_target="tpu_custom_call" | custom-call | flops 8589934592 | bytes 18874368 | tf_op jit(solution)/shard_map/pallas_call | solution.py:152
  84.8 1.3 copy-done.4
  86.1 0.1 add_bitcast_fusion
  86.3 0.2 copy.24
  86.5 0.0 collective-permute-done
  86.6 0.0 copy-start.3
  86.6 1.0 copy-done.3
  87.6 14.2 %shard_map.129 = (bf16[1024,1024]{1,0:T(8,128)(2,1)}, bf16[2,8,144,128]{3,2,1,0:T(8,128)(2,1)S(1)}) custom-call(bf16[1024,1024]{1,0:T(8,128)(2,1)} %copy-done.1, bf16[32,1024]{1,0:T(8,128)(2,1)S(1)} %pad_maximum_fusion.halo_ref, f32[4,1024]{1,0:T(4,128)S(1)} %copy-done.5, bf16[1024,256]{1,0:T(8,128)(2,1)S(1)} %get-tuple-element.10.b_ref.c_ref, ...), custom_call_target="tpu_custom_call" | custom-call | tf_op jit(solution)/shard_map/pallas_call | solution.py:568
  101.8 18.7 %shard_map.132.enter_ref = bf16[2,8,128,128]{3,2,1,0:T(8,128)(2,1)S(1)} custom-call(bf16[2,8,144,128]{3,2,1,0:T(8,128)(2,1)S(1)} %get-tuple-element.12.packed_ref), custom_call_target="tpu_custom_call" | custom-call | tf_op jit(solution)/shard_map/pallas_call | solution.py:351
  120.6 1.6 copy-done.7
  122.2 11.7 %shard_map.130.y_ref = f32[1024,1024]{1,0:T(8,128)} custom-call(f32[8]{0:T(128)S(1)} %copy-done.11, bf16[1024,1024]{1,0:T(8,128)(2,1)S(1)} %copy-done.7, bf16[1024,256]{1,0:T(8,128)(2,1)S(1)} %get-tuple-element.10.b_ref.c_ref, bf16[1024,256]{1,0:T(8,128)(2,1)S(1)} %get-tuple-element.10.b_ref.c_ref, f32[1024,8]{1,0:T(8,128)S(1)} %bitcast.34, ...), custom_call_target="tpu_custom_call" | custom-call | flops 2147483648 | bytes 8388608 | tf_op jit(solution)/shard_map/pallas_call | solution.py:592
  133.9 11.2 %shard_map.133.normed_ref = bf16[512,2048]{1,0:T(8,128)(2,1)S(1)} custom-call(f32[1024,1024]{1,0:T(8,128)} %shard_map.130.y_ref, bf16[1024,256]{1,0:T(8,128)(2,1)S(1)} %get-tuple-element.10.b_ref.c_ref, f32[1024,8]{1,0:T(8,128)S(1)} %bitcast.35, bf16[1024,1024]{1,0:T(8,128)(2,1)} %copy-done.4, f32[1,1024]{1,0:T(1,128)S(1)} %bitcast.37, ...), custom_call_target="tpu_custom_call" | custom-call | tf_op jit(solution)/shard_map/pallas_call | solution.py:615
  145.1 0.0 copy-start.12
  145.1 41.9 %shard_map.134 = f32[512,512]{1,0:T(8,128)S(1)} custom-call(bf16[512,2048]{1,0:T(8,128)(2,1)S(1)} %shard_map.133.normed_ref, bf16[1024,4096]{1,0:T(8,128)(2,1)} %table_ref.1, s32[1,4096]{1,0:T(1,128)S(1)} %bitcast.39), custom_call_target="tpu_custom_call" | custom-call | flops 25769803776 | bytes 10485760 | tf_op jit(solution)/shard_map/pallas_call | solution.py:493
  187.1 1.0 multiply_convert_fusion
  (32 shorter events, 0.2 us)
Async XLA Ops:
  0.0 61.9 %copy-start = (bf16[4096,8]{0,1:T(8,128)(2,1)S(1)}, bf16[4096,8]{0,1:T(8,128)(2,1)}, u32[]{:S(2)}) copy-start(bf16[4096,8]{0,1:T(8,128)(2,1)} %param.17) | copy-start | bytes 196612
  0.0 1.1 copy-start.8
  1.1 0.7 copy-start.9
  39.8 22.1 %copy-start.14 = (f32[8]{0:T(128)S(1)}, f32[8]{0:T(128)}, u32[]{:S(2)}) copy-start(f32[8]{0:T(128)} %param.18) | copy-start | bytes 100
  39.9 22.1 %copy-start.15 = (bf16[1024,4096]{1,0:T(8,128)(2,1)S(1)}, bf16[1024,4096]{1,0:T(8,128)(2,1)}, u32[]{:S(2)}) copy-start(bf16[1024,4096]{1,0:T(8,128)(2,1)} %shard_map.127.a_ref) | copy-start | bytes 25165828
  56.8 28.0 %copy-start.1 = (bf16[1024,1024]{1,0:T(8,128)(2,1)}, bf16[1024,1024]{1,0:T(8,128)(2,1)S(1)}, u32[]{:S(2)}) copy-start(bf16[1024,1024]{1,0:T(8,128)(2,1)S(1)} %get-tuple-element.9.value_ref) | copy-start | bytes 6291460
  56.8 7.8 %copy-start.13 = (f32[8]{0:T(128)S(1)}, f32[8]{0:T(128)}, u32[]{:S(2)}) copy-start(f32[8]{0:T(128)} %param.19) | copy-start | bytes 100
  56.8 29.7 %collective-permute-start = (bf16[16,1024]{1,0:T(8,128)(2,1)S(1)}, bf16[16,1024]{1,0:T(8,128)(2,1)S(1)}, u32[]{:S(2)}, u32[]{:S(2)}) collective-permute-start(bf16[16,1024]{1,0:T(8,128)(2,1)S(1)} %get-tuple-element.13), channel_id=1, source_target_pairs={{0,8},{8,16},{16,24},{1,9},{9,17},{17,25},{2,10},{10,18},{18,26},{... | collective-permute-start | bytes 98312 | tf_op jit(solution)/shard_map/ppermute | solution.py:277
  60.4 26.1 %collective-permute-start.1 = (bf16[16,1024]{1,0:T(8,128)(2,1)S(1)}, bf16[16,1024]{1,0:T(8,128)(2,1)S(1)}, u32[]{:S(2)}, u32[]{:S(2)}) collective-permute-start(bf16[16,1024]{1,0:T(8,128)(2,1)S(1)} %get-tuple-element.14), channel_id=1, source_target_pairs={{8,0},{16,8},{24,16},{9,1},{17,9},{25,17},{10,2},{18,10},{26,18},{... | collective-permute-start | bytes 98312 | tf_op jit(solution)/shard_map/ppermute | solution.py:277
  64.4 20.4 %copy-start.2 = (f32[1024,8]{1,0:T(8,128)}, f32[1024,8]{1,0:T(8,128)S(1)}, u32[]{:S(2)}) copy-start(f32[1024,8]{1,0:T(8,128)S(1)} %compare_select_fusion.step_ref) | copy-start | bytes 98308
  71.1 15.5 %copy-start.5 = (f32[4,1024]{1,0:T(4,128)S(1)}, f32[4,1024]{1,0:T(4,128)}, u32[]{:S(2)}) copy-start(f32[4,1024]{1,0:T(4,128)} %taps_ref.1) | copy-start | bytes 49156
  71.1 49.5 %copy-start.11 = (f32[8]{0:T(128)S(1)}, f32[8]{0:T(128)}, u32[]{:S(2)}) copy-start(f32[8]{0:T(128)} %skip_ref.1) | copy-start | bytes 100
  84.8 1.3 copy-start.4
  86.1 47.8 %copy-start.6 = (f32[1024]{0:T(1024)S(1)}, f32[1024]{0:T(1024)}, u32[]{:S(2)}) copy-start(f32[1024]{0:T(1024)} %param.22) | copy-start | bytes 12292
  86.6 1.0 copy-start.3
  120.6 1.6 copy-start.7
  122.1 23.0 %copy-start.10 = (s32[4096]{0:T(1024)S(1)}, s32[4096]{0:T(1024)}, u32[]{:S(2)}) copy-start(s32[4096]{0:T(1024)} %param.24) | copy-start | bytes 49156
  145.1 41.9 %copy-start.12 = (s32[512,512]{1,0:T(8,128)S(1)}, s32[512,512]{1,0:T(8,128)}, u32[]{:S(2)}) copy-start(s32[512,512]{1,0:T(8,128)} %param.25) | copy-start | bytes 3145732

commit v4 on v3

--- a/solution.py
+++ b/solution.py
@@ -169,8 +169,7 @@
     return 0.5 * v * (1.0 + jnp.tanh(0.5 * v))
 
 
-def column_of(ref, head):
-    values = ref[...]
+def column_of(values, head):
     lanes = lax.broadcasted_iota(jnp.int32, values.shape, 1)
     return jnp.sum(jnp.where(lanes == head, values, 0.0), axis=1, keepdims=True)
 
@@ -181,8 +180,8 @@
     nstate = b_ref.shape[1]
     value = value_ref[...].astype(F32)
     halo = halo_ref[...].astype(F32)
-    step = column_of(step_ref, head)
-    cum = column_of(cum_ref, head)
+    step = column_of(step_ref[...], head)
+    cum = column_of(cum_ref[...], head)
 
     def finish(conv, end):
         xs = silu(conv).astype(BF16)
@@ -215,71 +214,33 @@
         finish(conv, cum[0:1])
 
 
-def local_body(skip_ref, xs_ref, b_ref, c_ref, cum_ref, step_row_ref, cum_row_ref, y_ref, scores):
-    branch, head = pl.program_id(0), pl.program_id(1)
-    rows = xs_ref.shape[0]
-
-    @pl.when(head == 0)
-    def _():
-        scores[...] = lax.dot_general(
-            c_ref[...], b_ref[...], (((1,), (1,)), ((), ())), preferred_element_type=F32
-        )
-
-    cum = column_of(cum_ref, head)
-    cum_row = cum_row_ref[0]
-    step_row = step_row_ref[0]
-    xs = xs_ref[...]
-    skip = skip_ref[head]
+def step_body(raw_ref, bias_ref, rate_ref, step_ref, cum_ref):
+    rows = raw_ref.shape[0] // 2
+    order = lax.broadcasted_iota(jnp.int32, (rows, rows), 0) - lax.broadcasted_iota(
+        jnp.int32, (rows, rows), 1
+    )
+    for branch in (0, 1):
+        part = pl.ds(branch * rows, rows)
+        raw = raw_ref[part, :] + bias_ref[...]
+        step = jnp.maximum(raw, 0.0) + jnp.log1p(jnp.exp(-jnp.abs(raw)))
+        summed = jnp.where(order >= 0 if branch == 0 else order <= 0, 1.0, 0.0)
+        step_ref[part, :] = step
+        cum_ref[part, :] = jnp.dot(
+            summed,
+            -step * rate_ref[...],
+            precision=lax.Precision.HIGHEST,
+            preferred_element_type=F32,
+        )
+
+
+def scan_body(
+    skip_ref, packed_ref, xs_ref, bc_ref, cum_ref, step_row_ref, cum_row_ref, gate_ref, gain_ref,
+    out_ref, scores, local, inbox, outbox, send_sem, recv_sem,
+):
+    heads = packed_ref.shape[1]
+    nstate, head_dim = inbox.shape[2:]
+    rows = out_ref.shape[0]
     size = min(TILE, rows)
-    below = lax.broadcasted_iota(jnp.int32, (size, size), 0) - lax.broadcasted_iota(
-        jnp.int32, (size, size), 1
-    )
-
-    def run(sign):
-        for t in range(0, rows, size):
-            at = slice(t, t + size)
-            total = xs[at].astype(F32) * skip
-            for s in range(0, rows, size):
-                if sign * (t - s) < 0:
-                    continue
-                gaps = cum[at] - cum_row[:, s : s + size]
-                if s == t:
-                    gaps = jnp.where(sign * below >= 0, gaps, -jnp.inf)
-                mixing = jnp.exp(gaps) * (scores[at, s : s + size] * step_row[:, s : s + size])
-                total += jnp.dot(
-                    mixing.astype(BF16), xs[s : s + size], preferred_element_type=F32
-                )
-            y_ref[at, :] = total
-
-    @pl.when(branch == 0)
-    def _():
-        run(1)
-
-    @pl.when(branch == 1)
-    def _():
-        run(-1)
-
-
-def norm_body(y_ref, c_ref, cum_ref, gate_ref, gain_ref, enter_ref, out_ref):
-    head = pl.program_id(1)
-    cum = column_of(cum_ref, head)
-    carried = jnp.dot(c_ref[...], enter_ref[0, 0], preferred_element_type=F32)
-    y = y_ref[...] + jnp.exp(cum) * carried
-    gate = gate_ref[...].astype(F32)
-    gated = y * silu(gate)
-    mean = jnp.mean(gated * gated, axis=1, keepdims=True)
-    out_ref[...] = (gated * lax.rsqrt(mean + 1e-05) * gain_ref[...]).astype(BF16)
-
-
-def shift(block, distance):
-    count = lax.axis_size("seq")
-    route = [(i, i + distance) for i in range(count) if 0 <= i + distance < count]
-    return lax.ppermute(block, "seq", route)
-
-
-def chain_body(packed_ref, enter_ref, inbox, outbox, send_sem, recv_sem):
-    heads = packed_ref.shape[1]
-    nstate = inbox.shape[2]
     count = lax.axis_size("seq")
     place = lax.axis_index("seq")
     toward = [(place + 1) % count, (place + count - 1) % count]
@@ -309,32 +270,97 @@
 
     def relay(branch, head):
         copy(branch, head).wait_recv()
-        arrived = inbox[branch, head]
-        enter_ref[branch, head] = arrived
 
         @pl.when(jnp.logical_not(last[branch]))
         def _():
             decay = packed_ref[branch, head, nstate : nstate + 1, :].astype(F32)
             end = packed_ref[branch, head, :nstate, :].astype(F32)
-            outbox[branch, head] = (decay * arrived.astype(F32) + end).astype(BF16)
+            arrived = inbox[branch, head].astype(F32)
+            outbox[branch, head] = (decay * arrived + end).astype(BF16)
             copy(branch, head).start()
+
+    def lanes(head):
+        return pl.ds(pl.multiple_of(head * head_dim, head_dim), head_dim)
+
+    def within(branch):
+        base = branch * rows
+        part = pl.ds(base, rows)
+        scores[...] = lax.dot_general(
+            bc_ref[part, nstate:],
+            bc_ref[part, :nstate],
+            (((1,), (1,)), ((), ())),
+            preferred_element_type=F32,
+        )
+        sign = 1 - 2 * branch
+        below = lax.broadcasted_iota(jnp.int32, (size, size), 0) - lax.broadcasted_iota(
+            jnp.int32, (size, size), 1
+        )
+
+        def one(head, carry):
+            cum = column_of(cum_ref[part, :], head)
+            cum_row = cum_row_ref[branch * heads + head]
+            step_row = step_row_ref[branch * heads + head]
+            skip = skip_ref[head]
+            xs = xs_ref[part, lanes(head)]
+            for t in range(0, rows, size):
+                at = slice(t, t + size)
+                total = xs[at].astype(F32) * skip
+                for s in range(0, rows, size):
+                    if sign * (t - s) < 0:
+                        continue
+                    gaps = cum[at] - cum_row[:, s : s + size]
+                    if s == t:
+                        gaps = jnp.where(sign * below >= 0, gaps, -jnp.inf)
+                    mixing = jnp.exp(gaps) * (scores[at, s : s + size] * step_row[:, s : s + size])
+                    total += jnp.dot(
+                        mixing.astype(BF16), xs[s : s + size], preferred_element_type=F32
+                    )
+                local[base + t : base + t + size, lanes(head)] = total
+            return carry
+
+        lax.fori_loop(0, heads, one, 0)
+
+    def normalize(branch):
+        part = pl.ds(branch * rows, rows)
+
+        def one(head, carry):
+            cum = column_of(cum_ref[part, :], head)
+            carried = jnp.dot(
+                bc_ref[part, nstate:], inbox[branch, head], preferred_element_type=F32
+            )
+            y = local[part, lanes(head)] + jnp.exp(cum) * carried
+            gated = y * silu(gate_ref[part, lanes(head)].astype(F32))
+            mean = jnp.mean(gated * gated, axis=1, keepdims=True)
+            normed = gated * lax.rsqrt(mean + 1e-05) * gain_ref[:, lanes(head)]
+            out_ref[:, lanes(branch * heads + head)] = normed.astype(BF16)
+            return carry
+
+        lax.fori_loop(0, heads, one, 0)
 
     for branch in (0, 1):
 
         @pl.when(first[branch])
         def _(branch=branch):
             for head in range(heads):
-                enter_ref[branch, head] = jnp.zeros(inbox.shape[2:], BF16)
+                inbox[branch, head] = jnp.zeros(inbox.shape[2:], BF16)
                 outbox[branch, head] = packed_ref[branch, head, :nstate, :]
                 copy(branch, head).start()
 
-    for near, order in ((2 * place < count, (0, 1)), (2 * place >= count, (1, 0))):
-        for branch in order:
-
-            @pl.when(near & jnp.logical_not(first[branch]))
-            def _(branch=branch):
-                for head in range(heads):
-                    relay(branch, head)
+    def relays(near, branch):
+        @pl.when(near & jnp.logical_not(first[branch]))
+        def _():
+            for head in range(heads):
+                relay(branch, head)
+
+    forward_near, reverse_near = 2 * place < count, 2 * place >= count
+    relays(forward_near, 0)
+    relays(reverse_near, 1)
+    within(0)
+    relays(forward_near, 1)
+    relays(reverse_near, 0)
+    within(1)
+    normalize(0)
+    normalize(1)
 
     for branch in (0, 1):
 
@@ -344,25 +370,10 @@
                 copy(branch, head).wait_send()
 
 
-def entering(packed, nstate):
-    _, heads, _, head_dim = packed.shape
-    shape = (2, heads, nstate, head_dim)
-    vmem = pl.BlockSpec(memory_space=pltpu.VMEM)
-    return pl.pallas_call(
-        chain_body,
-        in_specs=[vmem],
-        out_specs=vmem,
-        out_shape=jax.ShapeDtypeStruct(shape, BF16),
-        scratch_shapes=[
-            pltpu.VMEM(shape, BF16),
-            pltpu.VMEM(shape, BF16),
-            pltpu.SemaphoreType.DMA((2, heads)),
-            pltpu.SemaphoreType.DMA((2, heads)),
-        ],
-        compiler_params=pltpu.CompilerParams(
-            collective_id=1, has_side_effects=True, vmem_limit_bytes=VMEM_LIMIT
-        ),
-    )(packed)
+def shift(block, distance):
+    count = lax.axis_size("seq")
+    route = [(i, i + distance) for i in range(count) if 0 <= i + distance < count]
+    return lax.ppermute(block, "seq", route)
 
 
 def flip(me, bit):
@@ -547,23 +558,21 @@
         [shift(value[rows - HALO : rows], 1), shift(value[rows : rows + HALO], -1)], axis=0
     )
     step_raw = jnp.dot(both, step_proj, preferred_element_type=F32)
-    step = jax.nn.softplus(step_raw + step_bias).reshape(2, rows, heads)
-    log_decay = -step * decay_rate
-    cum = jnp.stack(
-        [jnp.cumsum(log_decay[0], axis=0), lax.cumsum(log_decay[1], axis=0, reverse=True)]
-    )
-    step_rows = jnp.swapaxes(step, 1, 2).reshape(2 * heads, 1, rows)
-    cum_rows = jnp.swapaxes(cum, 1, 2).reshape(2 * heads, 1, rows)
-    step = step.reshape(2 * rows, heads)
-    cum = cum.reshape(2 * rows, heads)
+    per_step = jax.ShapeDtypeStruct((2 * rows, heads), F32)
+    step, cum = pl.pallas_call(
+        step_body, out_shape=[per_step, per_step], compiler_params=params(0)
+    )(step_raw, step_bias[None, :], decay_rate[None, :])
+
+    def as_rows(a):
+        return jnp.swapaxes(a.reshape(2, rows, heads), 1, 2).reshape(2 * heads, 1, rows)
+
+    step_rows, cum_rows = as_rows(step), as_rows(cum)
     (gate,) = products(both, (gate_proj,))
 
     grid = (2, heads)
     block = pl.BlockSpec((rows, head_dim), lambda b, h: (b, h))
     b_block = pl.BlockSpec((rows, nstate), lambda b, h: (b, 0))
-    c_block = pl.BlockSpec((rows, nstate), lambda b, h: (b, 1))
     column = pl.BlockSpec((rows, heads), lambda b, h: (b, 0))
-    row = pl.BlockSpec((1, 1, rows), lambda b, h: (b * heads + h, 0, 0))
 
     xs, packed = pl.pallas_call(
         state_body,
@@ -587,46 +596,30 @@
         compiler_params=params(2),
     )(value, halo, conv_kernel, bc, step, cum)
 
-    enter = entering(packed, nstate)
-
-    y = pl.pallas_call(
-        local_body,
-        grid=grid,
-        in_specs=[
-            pl.BlockSpec(memory_space=pltpu.SMEM),
-            block,
-            b_block,
-            c_block,
-            column,
-            row,
-            row,
+    vmem = pl.BlockSpec(memory_space=pltpu.VMEM)
+    states = (2, heads, nstate, head_dim)
+    normed = pl.pallas_call(
+        scan_body,
+        in_specs=[pl.BlockSpec(memory_space=pltpu.SMEM)] + [vmem] * 8,
+        out_specs=vmem,
+        out_shape=jax.ShapeDtypeStruct((rows, 2 * inner), BF16),
+        scratch_shapes=[
+            pltpu.VMEM((rows, rows), F32),
+            pltpu.VMEM((2 * rows, inner), F32),
+            pltpu.VMEM(states, BF16),
+            pltpu.VMEM(states, BF16),
+            pltpu.SemaphoreType.DMA((2, heads)),
+            pltpu.SemaphoreType.DMA((2, heads)),
         ],
-        out_specs=block,
-        out_shape=jax.ShapeDtypeStruct((2 * rows, inner), F32),
-        scratch_shapes=[pltpu.VMEM((rows, rows), F32)],
-        compiler_params=params(2),
+        compiler_params=pltpu.CompilerParams(
+            collective_id=1, has_side_effects=True, vmem_limit_bytes=VMEM_LIMIT
+        ),
         cost_estimate=pl.CostEstimate(
             flops=8 * rows * rows * inner,
             bytes_accessed=16 * rows * inner,
             transcendentals=2 * heads * rows * rows,
         ),
-    )(skip_gain, xs, bc, bc, cum, step_rows, cum_rows)
-
-    normed = pl.pallas_call(
-        norm_body,
-        grid=grid,
-        in_specs=[
-            block,
-            c_block,
-            column,
-            block,
-            pl.BlockSpec((1, head_dim), lambda b, h: (0, h)),
-            pl.BlockSpec((1, 1, nstate, head_dim), lambda b, h: (b, h, 0, 0)),
-        ],
-        out_specs=pl.BlockSpec((rows, head_dim), lambda b, h: (0, b * heads + h)),
-        out_shape=jax.ShapeDtypeStruct((rows, 2 * inner), BF16),
-        compiler_params=params(2),
-    )(y, bc, cum, gate, norm_gain[None, :], enter)
+    )(skip_gain, packed, xs, bc, cum, step_rows, cum_rows, gate, norm_gain[None, :])
 
     summed = output_sum(normed, out_proj, partner, tokens.shape[1])
     return (summed * keep_mask.astype(F32) * (1.0 / 0.9)).astype(BF16)

time: 189 us -> 171 us (0.905)
  Pallas kernels: 166 us -> 159 us
  other arithmetic: 7.38 us -> 1.06 us
  local copies, waits for them, and re-layouts: 6.48 us -> 2.28 us
    pallas_call x3 -> x2, Pallas kernels: 41.7 us -> 34 us  [the longest x1 32.1 us: shards(): pl.pallas_call(scan_body, in_specs=[pl.BlockSpec(memory_space=pltpu.SMEM)...]
    another operation x5 -> x0, other arithmetic: 6.24 us -> none
    unnamed x32 -> x28, local copies, waits for them, and re-layouts: 5.77 us -> 1.86 us
  transfers between devices with their start and end apart: 2 -> 2, of which waited for: 0 -> 0; matrix products, arithmetic and copies ran while one was open for 5% -> 2% of each run, Pallas kernels for 7% -> 10%
where the time goes in v4:
time: 171 us
  Pallas kernels  159 us (93%)
  starting transfers between devices  5.23 us (3%)
  matrix products  2.3 us (1%)
  local copies, waits for them, and re-layouts  2.28 us (1%)
    pallas_call x1, Pallas kernels, output_sum(): pl.pallas_call(output_body, in_specs=[vmem] * 3, out_specs=vmem, out_shap...  41.9 us
    pallas_call x1, Pallas kernels, gather_both(): pl.pallas_call(gather_body, in_specs=[vmem] * 2, out_specs=vmem, out_shap...  38.1 us
    pallas_call x1, Pallas kernels, shards(): pl.pallas_call(scan_body, in_specs=[pl.BlockSpec(memory_space=pltpu.SMEM)...  32.1 us
    pallas_call x2, Pallas kernels, products(): pl.pallas_call(functools.partial(product_body, counts), grid=(steps,), in...  31.1 us
    pallas_call x1, Pallas kernels, shards(): pl.pallas_call(state_body, grid=grid, in_specs=[block, pl.BlockSpec((HALO...  14.2 us
    ppermute x2, starting transfers between devices, shift(): return lax.ppermute(block, 'seq', route)  5.23 us
  transfers between devices with their start and end apart: 2, of which 0 were waited for; matrix products, arithmetic and copies ran while one was open for 2% of the time, Pallas kernels for 10%

profile of v4, /device:TPU:0, one launch (start us, length us, event | category | flops | bytes accessed | tf_op | source)
XLA Modules:
  0.0 170.5 jit_solution(8481235356398458609)
XLA Ops:
  0.0 1.1 copy-done.8
  1.1 0.7 copy-done.9
  1.8 38.1 %shard_map.127.a_ref = bf16[1024,4096]{1,0:T(8,128)(2,1)} custom-call(bf16[512,512]{1,0:T(8,128)(2,1)S(1)} %copy-done.8, s32[1,4096]{1,0:T(1,128)S(1)} %bitcast.15), custom_call_target="tpu_custom_call" | custom-call | flops 17179869184 | bytes 12582912 | tf_op jit(solution)/shard_map/pallas_call | solution.py:113
  39.9 16.7 %shard_map.128 = (bf16[1024,1024]{1,0:T(8,128)(2,1)S(1)}, bf16[1024,256]{1,0:T(8,128)(2,1)S(1)}) custom-call(bf16[1024,4096]{1,0:T(8,128)(2,1)} %shard_map.127.a_ref, bf16[4096,1024]{1,0:T(8,128)(2,1)} %refs_0_.2, bf16[4096,256]{1,0:T(8,128)(2,1)} %refs_1_.1), custom_call_target="tpu_custom_call" | custom-call | flops 10737418240 | bytes 21495808 | tf_op jit(solution)/shard_map/pallas_call | solution.py:152
  56.6 0.0 copy-start.1
  56.6 3.5 %collective-permute-start = (bf16[16,1024]{1,0:T(8,128)(2,1)S(1)}, bf16[16,1024]{1,0:T(8,128)(2,1)S(1)}, u32[]{:S(2)}, u32[]{:S(2)}) collective-permute-start(bf16[16,1024]{1,0:T(8,128)(2,1)S(1)} %get-tuple-element.17), channel_id=1, source_target_pairs={{0,8},{8,16},{16,24},{1,9},{9,17},{17,25},{2,10},{10,18},{18,26},{... | collective-permute-start | bytes 98312 | tf_op jit(solution)/shard_map/ppermute | solution.py:376
  60.1 0.0 slice-start
  60.2 0.0 slice-start.1
  60.2 1.7 %collective-permute-start.1 = (bf16[16,1024]{1,0:T(8,128)(2,1)S(1)}, bf16[16,1024]{1,0:T(8,128)(2,1)S(1)}, u32[]{:S(2)}, u32[]{:S(2)}) collective-permute-start(bf16[16,1024]{1,0:T(8,128)(2,1)S(1)} %get-tuple-element.18), channel_id=1, source_target_pairs={{8,0},{16,8},{24,16},{9,1},{17,9},{25,17},{10,2},{18,10},{26,18},{... | collective-permute-start | bytes 98312 | tf_op jit(solution)/shard_map/ppermute | solution.py:376
  61.9 14.4 %shard_map.131.gate_ref = bf16[1024,1024]{1,0:T(8,128)(2,1)S(1)} custom-call(bf16[1024,4096]{1,0:T(8,128)(2,1)} %shard_map.127.a_ref, bf16[4096,1024]{1,0:T(8,128)(2,1)} %refs_0_.3), custom_call_target="tpu_custom_call" | custom-call | flops 8589934592 | bytes 18874368 | tf_op jit(solution)/shard_map/pallas_call | solution.py:152
  76.4 0.0 copy-start.6
  76.4 0.0 copy-start.7
  76.4 0.0 copy-start.3
  76.4 0.0 copy-start.4
  76.4 0.0 copy-start.5
  76.4 2.3 %fusion.1.raw_ref = f32[1024,8]{1,0:T(8,128)S(1)} fusion(bf16[1024,4096]{1,0:T(8,128)(2,1)S(1)} %bitcast.20, bf16[4096,8]{0,1:T(8,128)(2,1)S(1)} %copy-done), kind=kOutput, calls=%fused_computation.3 | convolution fusion | flops 67108864 | bytes 8486912 | tf_op jit(solution)/shard_map/dot_general | solution.py:560
  78.7 0.0 copy-start.10
  78.7 0.0 copy-done.2
  78.8 0.0 copy-done.6
  78.8 0.0 copy-done.7
  78.8 1.9 %shard_map.129 = (f32[1024,8]{1,0:T(8,128)S(1)}, f32[1024,8]{1,0:T(8,128)S(1)}) custom-call(f32[1024,8]{1,0:T(8,128)S(1)} %fusion.1.raw_ref, f32[1,8]{1,0:T(1,128)S(1)} %bitcast.13, f32[1,8]{1,0:T(1,128)S(1)} %bitcast.14), custom_call_target="tpu_custom_call" | custom-call | tf_op jit(solution)/shard_map/pallas_call | solution.py:562
  80.7 0.2 copy.16
  80.9 0.1 reshape.15.cum_row_ref
  80.9 0.2 copy.15
  81.1 0.1 reshape.13.step_row_ref
  81.2 0.0 collective-permute-done
  81.2 0.0 collective-permute-done.1
  81.2 14.2 %shard_map.130 = (bf16[1024,1024]{1,0:T(8,128)(2,1)}, bf16[2,8,144,128]{3,2,1,0:T(8,128)(2,1)S(1)}) custom-call(bf16[1024,1024]{1,0:T(8,128)(2,1)} %copy-done.1, bf16[32,1024]{1,0:T(8,128)(2,1)S(1)} %pad_maximum_fusion.halo_ref, f32[4,1024]{1,0:T(4,128)S(1)} %copy-done.3, bf16[1024,256]{1,0:T(8,128)(2,1)S(1)} %get-tuple-element.12.b_ref.bc_ref, ...), custom_call_target="tpu_custom_call" | custom-call | tf_op jit(solution)/shard_map/pallas_call | solution.py:577
  95.4 32.1 %shard_map.132.normed_ref = bf16[512,2048]{1,0:T(8,128)(2,1)S(1)} custom-call(f32[8]{0:T(128)S(1)} %copy-done.5, bf16[2,8,144,128]{3,2,1,0:T(8,128)(2,1)S(1)} %get-tuple-element.15.packed_ref, bf16[1024,1024]{1,0:T(8,128)(2,1)} %get-tuple-element.16.xs_ref, bf16[1024,256]{1,0:T(8,128)(2,1)S(1)} %get-tuple-element.12.b_ref.bc_ref, ...), custom_call_target="tpu_custom_call" | custom-call | flops 2147483648 | bytes 8388608 | tf_op jit(solution)/shard_map/pallas_call | solution.py:601
  127.5 0.0 copy-start.11
  127.5 41.9 %shard_map.133 = f32[512,512]{1,0:T(8,128)S(1)} custom-call(bf16[512,2048]{1,0:T(8,128)(2,1)S(1)} %shard_map.132.normed_ref, bf16[1024,4096]{1,0:T(8,128)(2,1)} %table_ref.1, s32[1,4096]{1,0:T(1,128)S(1)} %bitcast.16), custom_call_target="tpu_custom_call" | custom-call | flops 25769803776 | bytes 10485760 | tf_op jit(solution)/shard_map/pallas_call | solution.py:504
  169.5 1.0 multiply_convert_fusion
  (16 shorter events, 0.0 us)
Async XLA Ops:
  0.0 76.3 %copy-start = (bf16[4096,8]{0,1:T(8,128)(2,1)S(1)}, bf16[4096,8]{0,1:T(8,128)(2,1)}, u32[]{:S(2)}) copy-start(bf16[4096,8]{0,1:T(8,128)(2,1)} %param.17) | copy-start | bytes 196612
  0.0 1.1 copy-start.8
  1.1 0.7 copy-start.9
  56.6 19.7 %copy-start.1 = (bf16[1024,1024]{1,0:T(8,128)(2,1)}, bf16[1024,1024]{1,0:T(8,128)(2,1)S(1)}, u32[]{:S(2)}) copy-start(bf16[1024,1024]{1,0:T(8,128)(2,1)S(1)} %get-tuple-element.11.value_ref) | copy-start | bytes 6291460
  56.6 24.5 %collective-permute-start = (bf16[16,1024]{1,0:T(8,128)(2,1)S(1)}, bf16[16,1024]{1,0:T(8,128)(2,1)S(1)}, u32[]{:S(2)}, u32[]{:S(2)}) collective-permute-start(bf16[16,1024]{1,0:T(8,128)(2,1)S(1)} %get-tuple-element.17), channel_id=1, source_target_pairs={{0,8},{8,16},{16,24},{1,9},{9,17},{17,25},{2,10},{10,18},{18,26},{... | collective-permute-start | bytes 98312 | tf_op jit(solution)/shard_map/ppermute | solution.py:376
  60.1 16.2 %slice-start = ((s8[8388608]{0:T(1024)(128)(4,1)}), s8[4194304]{0:T(1024)(128)(4,1)S(1)}, s32[]{:S(2)}) async-start(s8[8388608]{0:T(1024)(128)(4,1)} %bitcast.19), calls=%async_computation | async-start | bytes 8388608
  60.2 16.2 %slice-start.1 = ((s8[8388608]{0:T(1024)(128)(4,1)}), s8[4194304]{0:T(1024)(128)(4,1)S(1)}, s32[]{:S(2)}) async-start(s8[8388608]{0:T(1024)(128)(4,1)} %bitcast.19), calls=%async_computation.1 | async-start | bytes 8388608
  60.2 21.0 %collective-permute-start.1 = (bf16[16,1024]{1,0:T(8,128)(2,1)S(1)}, bf16[16,1024]{1,0:T(8,128)(2,1)S(1)}, u32[]{:S(2)}, u32[]{:S(2)}) collective-permute-start(bf16[16,1024]{1,0:T(8,128)(2,1)S(1)} %get-tuple-element.18), channel_id=1, source_target_pairs={{8,0},{16,8},{24,16},{9,1},{17,9},{25,17},{10,2},{18,10},{26,18},{... | collective-permute-start | bytes 98312 | tf_op jit(solution)/shard_map/ppermute | solution.py:376
  76.4 2.4 %copy-start.2 = (bf16[1024,1024]{1,0:T(8,128)(2,1)}, bf16[1024,1024]{1,0:T(8,128)(2,1)S(1)}, u32[]{:S(2)}) copy-start(bf16[1024,1024]{1,0:T(8,128)(2,1)S(1)} %shard_map.131.gate_ref) | copy-start | bytes 6291460
  76.4 2.4 %copy-start.6 = (f32[8]{0:T(128)S(1)}, f32[8]{0:T(128)}, u32[]{:S(2)}) copy-start(f32[8]{0:T(128)} %param.18) | copy-start | bytes 100
  76.4 2.4 %copy-start.7 = (f32[8]{0:T(128)S(1)}, f32[8]{0:T(128)}, u32[]{:S(2)}) copy-start(f32[8]{0:T(128)} %param.19) | copy-start | bytes 100
  76.4 4.8 %copy-start.3 = (f32[4,1024]{1,0:T(4,128)S(1)}, f32[4,1024]{1,0:T(4,128)}, u32[]{:S(2)}) copy-start(f32[4,1024]{1,0:T(4,128)} %taps_ref.1) | copy-start | bytes 49156
  76.4 19.0 %copy-start.4 = (f32[1024]{0:T(1024)S(1)}, f32[1024]{0:T(1024)}, u32[]{:S(2)}) copy-start(f32[1024]{0:T(1024)} %param.22) | copy-start | bytes 12292
  76.4 19.0 %copy-start.5 = (f32[8]{0:T(128)S(1)}, f32[8]{0:T(128)}, u32[]{:S(2)}) copy-start(f32[8]{0:T(128)} %skip_ref.1) | copy-start | bytes 100
  78.7 48.8 %copy-start.10 = (s32[4096]{0:T(1024)S(1)}, s32[4096]{0:T(1024)}, u32[]{:S(2)}) copy-start(s32[4096]{0:T(1024)} %param.24) | copy-start | bytes 49156
  127.5 41.9 %copy-start.11 = (s32[512,512]{1,0:T(8,128)S(1)}, s32[512,512]{1,0:T(8,128)}, u32[]{:S(2)}) copy-start(s32[512,512]{1,0:T(8,128)} %param.25) | copy-start | bytes 3145732

commit v5 on v4

--- a/solution.py
+++ b/solution.py
@@ -28,6 +28,12 @@
     source = lax.broadcasted_iota(jnp.int32, (depth, partner.shape[1]), 0)
     source = source.astype(F32).astype(BF16)
     return jnp.where(source == local, jnp.ones((), BF16), jnp.zeros((), BF16))
+
+
+def chosen_deep(partner, low, depth):
+    return jnp.concatenate(
+        [chosen_rows(partner, low + part, DEPTH) for part in range(0, depth, DEPTH)], axis=0
+    )
 
 
 def gather_body(tokens_ref, partner_ref, out_ref, send_sem, recv_sem):
@@ -72,13 +78,12 @@
             partner = partner_ref[:, at(column)]
             part = jnp.zeros((rows, cols), F32)
             for owner in (block, flip(block, 1)):
-                for depth in range(0, cols, DEPTH):
-                    start = pl.multiple_of(owner * cols + depth, DEPTH)
-                    part += jnp.dot(
-                        out_ref[:rows, pl.ds(start, DEPTH)],
-                        chosen_rows(partner, start, DEPTH),
-                        preferred_element_type=F32,
-                    )
+                start = pl.multiple_of(owner * cols, cols)
+                part += jnp.dot(
+                    out_ref[:rows, pl.ds(start, cols)],
+                    chosen_deep(partner, start, cols),
+                    preferred_element_type=F32,
+                )
             if not initial:
                 part += out_ref[rows:, at(column)].astype(F32)
             out_ref[rows:, at(column)] = part.astype(BF16)
@@ -174,26 +179,24 @@
     return jnp.sum(jnp.where(lanes == head, values, 0.0), axis=1, keepdims=True)
 
 
-def state_body(value_ref, halo_ref, taps_ref, b_ref, step_ref, cum_ref, xs_ref, state_ref):
+def state_body(value_ref, halo_ref, taps_ref, b_ref, weight_ref, grown_ref, xs_ref, state_ref):
     branch, head = pl.program_id(0), pl.program_id(1)
     rows = value_ref.shape[0]
     nstate = b_ref.shape[1]
     value = value_ref[...].astype(F32)
     halo = halo_ref[...].astype(F32)
-    step = column_of(step_ref[...], head)
-    cum = column_of(cum_ref[...], head)
-
-    def finish(conv, end):
+    weight = column_of(weight_ref[...], head)
+
+    def finish(conv, last):
+        decay = column_of(grown_ref[last : last + 1, :], head)
         xs = silu(conv).astype(BF16)
         xs_ref[...] = xs
-        weighted = (xs.astype(F32) * (jnp.exp(end - cum) * step)).astype(BF16)
+        weighted = (xs.astype(F32) * weight).astype(BF16)
         state = lax.dot_general(
             b_ref[...], weighted, (((0,), (0,)), ((), ())), preferred_element_type=F32
         )
         state_ref[0, 0, :nstate, :] = state.astype(BF16)
-        state_ref[0, 0, nstate:, :] = jnp.broadcast_to(
-            jnp.exp(end), (HALO, state.shape[1])
-        ).astype(BF16)
+        state_ref[0, 0, nstate:, :] = jnp.broadcast_to(decay, (HALO, state.shape[1])).astype(BF16)
 
     @pl.when(branch == 0)
     def _():
@@ -202,7 +205,7 @@
         for k in range(KW - 1):
             low = HALO - (KW - 1) + k
             conv += taps_ref[k : k + 1, :] * ext[low : low + rows]
-        finish(conv, cum[rows - 1 : rows])
+        finish(conv, rows - 1)
 
     @pl.when(branch == 1)
     def _():
@@ -211,10 +214,10 @@
         for k in range(KW - 1):
             low = KW - 1 - k
             conv += taps_ref[k : k + 1, :] * ext[low : low + rows]
-        finish(conv, cum[0:1])
-
-
-def step_body(raw_ref, bias_ref, rate_ref, step_ref, cum_ref):
+        finish(conv, 0)
+
+
+def step_body(raw_ref, bias_ref, rate_ref, step_ref, cum_ref, weight_ref, grown_ref):
     rows = raw_ref.shape[0] // 2
     order = lax.broadcasted_iota(jnp.int32, (rows, rows), 0) - lax.broadcasted_iota(
         jnp.int32, (rows, rows), 1
@@ -225,16 +228,20 @@
         step = jnp.maximum(raw, 0.0) + jnp.log1p(jnp.exp(-jnp.abs(raw)))
         summed = jnp.where(order >= 0 if branch == 0 else order <= 0, 1.0, 0.0)
         step_ref[part, :] = step
-        cum_ref[part, :] = jnp.dot(
+        cum = jnp.dot(
             summed,
             -step * rate_ref[...],
             precision=lax.Precision.HIGHEST,
             preferred_element_type=F32,
         )
+        end = cum[rows - 1 : rows] if branch == 0 else cum[0:1]
+        cum_ref[part, :] = cum
+        weight_ref[part, :] = jnp.exp(end - cum) * step
+        grown_ref[part, :] = jnp.exp(cum)
 
 
 def scan_body(
-    skip_ref, packed_ref, xs_ref, bc_ref, cum_ref, step_row_ref, cum_row_ref, gate_ref, gain_ref,
+    skip_ref, packed_ref, xs_ref, bc_ref, cum_ref, grown_ref, step_row_ref, cum_row_ref, gate_ref, gain_ref,
     out_ref, scores, local, inbox, outbox, send_sem, recv_sem,
 ):
     heads = packed_ref.shape[1]
@@ -324,11 +331,11 @@
         part = pl.ds(branch * rows, rows)
 
         def one(head, carry):
-            cum = column_of(cum_ref[part, :], head)
+            grown = column_of(grown_ref[part, :], head)
             carried = jnp.dot(
                 bc_ref[part, nstate:], inbox[branch, head], preferred_element_type=F32
             )
-            y = local[part, lanes(head)] + jnp.exp(cum) * carried
+            y = local[part, lanes(head)] + grown * carried
             gated = y * silu(gate_ref[part, lanes(head)].astype(F32))
             mean = jnp.mean(gated * gated, axis=1, keepdims=True)
             normed = gated * lax.rsqrt(mean + 1e-05) * gain_ref[:, lanes(head)]
@@ -443,10 +450,11 @@
             part = jnp.dot(
                 normed_ref[:, :inner], table_ref[:, at(block)], preferred_element_type=F32
             )
-            for depth in range(0, width, DEPTH):
+            deep = min(4 * DEPTH, width)
+            for depth in range(0, width, deep):
                 part += jnp.dot(
-                    reverse[:, depth : depth + DEPTH],
-                    chosen_rows(partner, depth, DEPTH),
+                    reverse[:, depth : depth + deep],
+                    chosen_deep(partner, depth, deep),
                     preferred_element_type=F32,
                 )
             total[...] = part
@@ -559,8 +567,8 @@
     )
     step_raw = jnp.dot(both, step_proj, preferred_element_type=F32)
     per_step = jax.ShapeDtypeStruct((2 * rows, heads), F32)
-    step, cum = pl.pallas_call(
-        step_body, out_shape=[per_step, per_step], compiler_params=params(0)
+    step, cum, weight, grown = pl.pallas_call(
+        step_body, out_shape=[per_step] * 4, compiler_params=params(0)
     )(step_raw, step_bias[None, :], decay_rate[None, :])
 
     def as_rows(a):
@@ -594,13 +602,13 @@
             jax.ShapeDtypeStruct((2, heads, nstate + HALO, head_dim), BF16),
         ],
         compiler_params=params(2),
-    )(value, halo, conv_kernel, bc, step, cum)
+    )(value, halo, conv_kernel, bc, weight, grown)
 
     vmem = pl.BlockSpec(memory_space=pltpu.VMEM)
     states = (2, heads, nstate, head_dim)
     normed = pl.pallas_call(
         scan_body,
-        in_specs=[pl.BlockSpec(memory_space=pltpu.SMEM)] + [vmem] * 8,
+        in_specs=[pl.BlockSpec(memory_space=pltpu.SMEM)] + [vmem] * 9,
         out_specs=vmem,
         out_shape=jax.ShapeDtypeStruct((rows, 2 * inner), BF16),
         scratch_shapes=[
@@ -619,7 +627,7 @@
             bytes_accessed=16 * rows * inner,
             transcendentals=2 * heads * rows * rows,
         ),
-    )(skip_gain, packed, xs, bc, cum, step_rows, cum_rows, gate, norm_gain[None, :])
+    )(skip_gain, packed, xs, bc, cum, grown, step_rows, cum_rows, gate, norm_gain[None, :])
 
     summed = output_sum(normed, out_proj, partner, tokens.shape[1])
     return (summed * keep_mask.astype(F32) * (1.0 / 0.9)).astype(BF16)

time: 171 us -> 173 us (1.012)
  no operation moved by 1% of the time
where the time goes in v5:
time: 173 us
  Pallas kernels  160 us (92%)
  starting transfers between devices  5.22 us (3%)
  local copies, waits for them, and re-layouts  3.86 us (2%)
  matrix products  2.3 us (1%)
    pallas_call x1, Pallas kernels, output_sum(): pl.pallas_call(output_body, in_specs=[vmem] * 3, out_specs=vmem, out_shap...  41.9 us
    pallas_call x1, Pallas kernels, gather_both(): pl.pallas_call(gather_body, in_specs=[vmem] * 2, out_specs=vmem, out_shap...  38.1 us
    pallas_call x1, Pallas kernels, shards(): pl.pallas_call(scan_body, in_specs=[pl.BlockSpec(memory_space=pltpu.SMEM)...  33.3 us
    pallas_call x2, Pallas kernels, products(): pl.pallas_call(functools.partial(product_body, counts), grid=(steps,), in...  31.1 us
    pallas_call x1, Pallas kernels, shards(): pl.pallas_call(state_body, grid=grid, in_specs=[block, pl.BlockSpec((HALO...  13.3 us
    ppermute x2, starting transfers between devices, shift(): return lax.ppermute(block, 'seq', route)  5.22 us
  transfers between devices with their start and end apart: 2, of which 0 were waited for; matrix products, arithmetic and copies ran while one was open for 2% of the time, Pallas kernels for 10%

profile of v5, /device:TPU:0, one launch (start us, length us, event | category | flops | bytes accessed | tf_op | source)
XLA Modules:
  0.0 172.6 jit_solution(9858630996828517425)
XLA Ops:
  0.0 1.1 copy-done.9
  1.1 0.7 copy-done.10
  1.8 38.1 %shard_map.127.a_ref = bf16[1024,4096]{1,0:T(8,128)(2,1)} custom-call(bf16[512,512]{1,0:T(8,128)(2,1)S(1)} %copy-done.9, s32[1,4096]{1,0:T(1,128)S(1)} %bitcast.15), custom_call_target="tpu_custom_call" | custom-call | flops 17179869184 | bytes 12582912 | tf_op jit(solution)/shard_map/pallas_call | solution.py:118
  39.9 16.7 %shard_map.128 = (bf16[1024,1024]{1,0:T(8,128)(2,1)S(1)}, bf16[1024,256]{1,0:T(8,128)(2,1)S(1)}) custom-call(bf16[1024,4096]{1,0:T(8,128)(2,1)} %shard_map.127.a_ref, bf16[4096,1024]{1,0:T(8,128)(2,1)} %refs_0_.2, bf16[4096,256]{1,0:T(8,128)(2,1)} %refs_1_.1), custom_call_target="tpu_custom_call" | custom-call | flops 10737418240 | bytes 21495808 | tf_op jit(solution)/shard_map/pallas_call | solution.py:157
  56.6 0.0 copy-start.1
  56.7 3.5 %collective-permute-start = (bf16[16,1024]{1,0:T(8,128)(2,1)S(1)}, bf16[16,1024]{1,0:T(8,128)(2,1)S(1)}, u32[]{:S(2)}, u32[]{:S(2)}) collective-permute-start(bf16[16,1024]{1,0:T(8,128)(2,1)S(1)} %get-tuple-element.21), channel_id=1, source_target_pairs={{0,8},{8,16},{16,24},{1,9},{9,17},{17,25},{2,10},{10,18},{18,26},{... | collective-permute-start | bytes 98312 | tf_op jit(solution)/shard_map/ppermute | solution.py:383
  60.2 0.0 slice-start
  60.2 0.0 slice-start.1
  60.2 1.7 %collective-permute-start.1 = (bf16[16,1024]{1,0:T(8,128)(2,1)S(1)}, bf16[16,1024]{1,0:T(8,128)(2,1)S(1)}, u32[]{:S(2)}, u32[]{:S(2)}) collective-permute-start(bf16[16,1024]{1,0:T(8,128)(2,1)S(1)} %get-tuple-element.22), channel_id=1, source_target_pairs={{8,0},{16,8},{24,16},{9,1},{17,9},{25,17},{10,2},{18,10},{26,18},{... | collective-permute-start | bytes 98312 | tf_op jit(solution)/shard_map/ppermute | solution.py:383
  61.9 14.4 %shard_map.131.gate_ref = bf16[1024,1024]{1,0:T(8,128)(2,1)S(1)} custom-call(bf16[1024,4096]{1,0:T(8,128)(2,1)} %shard_map.127.a_ref, bf16[4096,1024]{1,0:T(8,128)(2,1)} %refs_0_.3), custom_call_target="tpu_custom_call" | custom-call | flops 8589934592 | bytes 18874368 | tf_op jit(solution)/shard_map/pallas_call | solution.py:157
  76.3 0.0 copy-done.1
  76.3 0.0 copy-done
  76.3 0.0 slice-done
  76.4 0.0 copy-start.7
  76.4 0.0 copy-start.8
  76.4 0.0 copy-start.4
  76.4 0.0 copy-start.5
  76.4 0.0 copy-start.6
  76.4 2.3 %fusion.1.raw_ref = f32[1024,8]{1,0:T(8,128)S(1)} fusion(bf16[1024,4096]{1,0:T(8,128)(2,1)S(1)} %bitcast.20, bf16[4096,8]{0,1:T(8,128)(2,1)S(1)} %copy-done), kind=kOutput, calls=%fused_computation.3 | convolution fusion | flops 67108864 | bytes 8486912 | tf_op jit(solution)/shard_map/dot_general | solution.py:568
  78.8 0.0 copy-start.11
  78.8 2.0 %shard_map.129 = (f32[1024,8]{1,0:T(8,128)S(1)}, f32[1024,8]{1,0:T(8,128)S(1)}, f32[1024,8]{1,0:T(8,128)S(1)}, f32[1024,8]{1,0:T(8,128)S(1)}) custom-call(f32[1024,8]{1,0:T(8,128)S(1)} %fusion.1.raw_ref, f32[1,8]{1,0:T(1,128)S(1)} %bitcast.13, f32[1,8]{1,0:T(1,128)S(1)} %bitcast.14), custom_call_target="tpu_custom_call" | custom-call | tf_op jit(solution)/shard_map/pallas_call | solution.py:570
  80.8 0.2 copy.15
  81.0 0.1 reshape.13.step_row_ref
  81.1 0.2 copy.16
  81.2 0.1 reshape.15.cum_row_ref
  81.3 0.0 collective-permute-done
  81.3 0.0 collective-permute-done.1
  81.3 13.3 %shard_map.130 = (bf16[1024,1024]{1,0:T(8,128)(2,1)}, bf16[2,8,144,128]{3,2,1,0:T(8,128)(2,1)S(1)}) custom-call(bf16[1024,1024]{1,0:T(8,128)(2,1)} %copy-done.1, bf16[32,1024]{1,0:T(8,128)(2,1)S(1)} %pad_maximum_fusion.halo_ref, f32[4,1024]{1,0:T(4,128)S(1)} %copy-done.4, bf16[1024,256]{1,0:T(8,128)(2,1)S(1)} %get-tuple-element.14.b_ref.bc_ref, ...), custom_call_target="tpu_custom_call" | custom-call | tf_op jit(solution)/shard_map/pallas_call | solution.py:585
  94.6 33.3 %shard_map.132.normed_ref = bf16[512,2048]{1,0:T(8,128)(2,1)} custom-call(f32[8]{0:T(128)S(1)} %copy-done.6, bf16[2,8,144,128]{3,2,1,0:T(8,128)(2,1)S(1)} %get-tuple-element.17.packed_ref, bf16[1024,1024]{1,0:T(8,128)(2,1)} %get-tuple-element.18.xs_ref, bf16[1024,256]{1,0:T(8,128)(2,1)S(1)} %get-tuple-element.14.b_ref.bc_ref, ...), custom_call_target="tpu_custom_call" | custom-call | flops 2147483648 | bytes 8388608 | tf_op jit(solution)/shard_map/pallas_call | solution.py:609
  128.0 1.6 copy-done.3
  129.6 41.9 %shard_map.133 = f32[512,512]{1,0:T(8,128)S(1)} custom-call(bf16[512,2048]{1,0:T(8,128)(2,1)S(1)} %copy-done.3, bf16[1024,4096]{1,0:T(8,128)(2,1)} %table_ref.1, s32[1,4096]{1,0:T(1,128)S(1)} %bitcast.16), custom_call_target="tpu_custom_call" | custom-call | flops 25769803776 | bytes 10485760 | tf_op jit(solution)/shard_map/pallas_call | solution.py:512
  171.5 1.0 multiply_convert_fusion
  (18 shorter events, 0.0 us)
Async XLA Ops:
  0.0 76.3 %copy-start = (bf16[4096,8]{0,1:T(8,128)(2,1)S(1)}, bf16[4096,8]{0,1:T(8,128)(2,1)}, u32[]{:S(2)}) copy-start(bf16[4096,8]{0,1:T(8,128)(2,1)} %param.17) | copy-start | bytes 196612
  0.0 1.1 copy-start.9
  1.1 0.7 copy-start.10
  56.6 19.7 %copy-start.1 = (bf16[1024,1024]{1,0:T(8,128)(2,1)}, bf16[1024,1024]{1,0:T(8,128)(2,1)S(1)}, u32[]{:S(2)}) copy-start(bf16[1024,1024]{1,0:T(8,128)(2,1)S(1)} %get-tuple-element.13.value_ref) | copy-start | bytes 6291460
  56.7 24.6 %collective-permute-start = (bf16[16,1024]{1,0:T(8,128)(2,1)S(1)}, bf16[16,1024]{1,0:T(8,128)(2,1)S(1)}, u32[]{:S(2)}, u32[]{:S(2)}) collective-permute-start(bf16[16,1024]{1,0:T(8,128)(2,1)S(1)} %get-tuple-element.21), channel_id=1, source_target_pairs={{0,8},{8,16},{16,24},{1,9},{9,17},{17,25},{2,10},{10,18},{18,26},{... | collective-permute-start | bytes 98312 | tf_op jit(solution)/shard_map/ppermute | solution.py:383
  60.2 16.2 %slice-start = ((s8[8388608]{0:T(1024)(128)(4,1)}), s8[4194304]{0:T(1024)(128)(4,1)S(1)}, s32[]{:S(2)}) async-start(s8[8388608]{0:T(1024)(128)(4,1)} %bitcast.19), calls=%async_computation | async-start | bytes 8388608
  60.2 16.2 %slice-start.1 = ((s8[8388608]{0:T(1024)(128)(4,1)}), s8[4194304]{0:T(1024)(128)(4,1)S(1)}, s32[]{:S(2)}) async-start(s8[8388608]{0:T(1024)(128)(4,1)} %bitcast.19), calls=%async_computation.1 | async-start | bytes 8388608
  60.2 21.1 %collective-permute-start.1 = (bf16[16,1024]{1,0:T(8,128)(2,1)S(1)}, bf16[16,1024]{1,0:T(8,128)(2,1)S(1)}, u32[]{:S(2)}, u32[]{:S(2)}) collective-permute-start(bf16[16,1024]{1,0:T(8,128)(2,1)S(1)} %get-tuple-element.22), channel_id=1, source_target_pairs={{8,0},{16,8},{24,16},{9,1},{17,9},{25,17},{10,2},{18,10},{26,18},{... | collective-permute-start | bytes 98312 | tf_op jit(solution)/shard_map/ppermute | solution.py:383
  76.4 2.4 %copy-start.2 = (bf16[1024,1024]{1,0:T(8,128)(2,1)}, bf16[1024,1024]{1,0:T(8,128)(2,1)S(1)}, u32[]{:S(2)}) copy-start(bf16[1024,1024]{1,0:T(8,128)(2,1)S(1)} %shard_map.131.gate_ref) | copy-start | bytes 6291460
  76.4 2.4 %copy-start.7 = (f32[8]{0:T(128)S(1)}, f32[8]{0:T(128)}, u32[]{:S(2)}) copy-start(f32[8]{0:T(128)} %param.18) | copy-start | bytes 100
  76.4 2.4 %copy-start.8 = (f32[8]{0:T(128)S(1)}, f32[8]{0:T(128)}, u32[]{:S(2)}) copy-start(f32[8]{0:T(128)} %param.19) | copy-start | bytes 100
  76.4 4.9 %copy-start.4 = (f32[4,1024]{1,0:T(4,128)S(1)}, f32[4,1024]{1,0:T(4,128)}, u32[]{:S(2)}) copy-start(f32[4,1024]{1,0:T(4,128)} %taps_ref.1) | copy-start | bytes 49156
  76.4 18.2 %copy-start.5 = (f32[1024]{0:T(1024)S(1)}, f32[1024]{0:T(1024)}, u32[]{:S(2)}) copy-start(f32[1024]{0:T(1024)} %param.22) | copy-start | bytes 12292
  76.4 18.2 %copy-start.6 = (f32[8]{0:T(128)S(1)}, f32[8]{0:T(128)}, u32[]{:S(2)}) copy-start(f32[8]{0:T(128)} %skip_ref.1) | copy-start | bytes 100
  78.8 49.2 %copy-start.11 = (s32[4096]{0:T(1024)S(1)}, s32[4096]{0:T(1024)}, u32[]{:S(2)}) copy-start(s32[4096]{0:T(1024)} %param.24) | copy-start | bytes 49156
  128.0 1.6 copy-start.3
  129.6 41.9 %copy-start.12 = (s32[512,512]{1,0:T(8,128)S(1)}, s32[512,512]{1,0:T(8,128)}, u32[]{:S(2)}) copy-start(s32[512,512]{1,0:T(8,128)} %param.25) | copy-start | bytes 3145732
